TPU v7x, 512 devices: a whole 4x8x8 slice. The times are simulated.
512 devices in a mesh: rep: 16 (over y, core), shard: 32 (over x, z).
Axes of the slice: x: 4, y: 8, z: 8, core: 2. Of those that a mesh axis runs over, the one named last changes fastest.
Arguments:
- weights: bfloat16 [16, 4096, 5120], P('rep', 'shard'), may hold values from -12 to 12
- warm_start: bfloat16 [16, 2, 16, 5120], P('rep'), may hold values from -4 to 4, as said below
Outputs:
- corrected: bfloat16 [16, 4096, 5120], P('rep', 'shard')
- factors: float32 [16, 2, 16, 5120], P('rep')
Inputs may be any that keep to these rules, and one draw needn't show every extreme that they name: `warm_start`: replicas whose indices differ only in bit 0 hold equal start vectors for matching 0, and replicas whose indices differ by 8 hold equal start vectors for matching 1.
All inputs are finite; a program needn't handle non-finite values.
Results may differ from a plain program's by a relative error of at most 0.0049.
Values sent between devices are 32-bit elements; how exact they have to be, the bound alone decides.
No kernel may reach another device: no remote copies, remote signals or barrier semaphores. Data moves between devices by JAX's collectives and lax.ppermute only.
A program may use at most 64 MiB of HBM per device.

v0:
```python
import jax
import jax.numpy as jnp
from jax import lax
from jax.sharding import PartitionSpec as P

STEPS = 2


def partner(value, axis, stride):
    return lax.ppermute(value, axis, [(i, i ^ 1 << stride) for i in range(lax.axis_size(axis))])


def shards(weights, warm_start):
    current = weights[0]
    replica = lax.axis_index("rep")
    half_rep = lax.axis_size("rep") // 2
    top_bit = lax.axis_size("rep").bit_length() - 2
    factor_list = []
    for matching in range(STEPS):
        if matching == 0:
            bit_number = 0
            parity = 1.0 - 2.0 * (replica % 2).astype(jnp.float32)
        else:
            bit_number = top_bit
            parity = 1.0 - 2.0 * (replica // half_rep).astype(jnp.float32)
        starts = warm_start[0, matching]
        sketch = lax.dot_general(
            starts, current, (((1,), (1,)), ((), ())), preferred_element_type=jnp.float32
        )
        sketch_other = partner(sketch, "rep", bit_number)
        differ = parity * (sketch - sketch_other)
        gram_local = lax.dot_general(
            differ, differ, (((1,), (1,)), ((), ())), precision=lax.Precision.HIGHEST
        )
        gram_sum = lax.psum(gram_local, "shard")
        triangle = jnp.linalg.cholesky(gram_sum)
        basis_rows = lax.linalg.triangular_solve(triangle, differ, left_side=True, lower=True)
        signed = parity * jnp.dot(
            basis_rows.astype(jnp.bfloat16), current, preferred_element_type=jnp.float32
        )
        summed = lax.psum(signed, "shard")
        factors = summed + partner(summed, "rep", bit_number)
        change = lax.dot_general(
            basis_rows, factors, (((0,), (0,)), ((), ())), precision=lax.Precision.HIGHEST
        )
        current = (current.astype(jnp.float32) - 0.5 * parity * change).astype(jnp.bfloat16)
        factor_list.append(factors)
    return (current[None], jnp.stack(factor_list)[None])


def solution(mesh):
    placed = (P("rep", "shard", None), P("rep", None, None, None))
    return jax.shard_map(
        shards,
        mesh=mesh,
        in_specs=placed,
        out_specs=(P("rep", "shard", None), P("rep", None, None, None)),
        check_vma=False,
    )
```

profile of v0, /device:TPU:16, one launch (start us, length us, event | category | flops | bytes accessed | tf_op | source)
XLA Modules:
  0.0 525.8 jit_solution(2069408081146969452)
XLA Ops:
  7.2 0.0 copy-start
  7.2 0.0 all-reduce.3.cloned.1.call-start
  7.2 1.9 fusion.4
  9.1 1.9 collective-permute-start
  11.1 1.1 collective-permute-done
  12.2 0.1 fusion.22
  12.3 81.9 %psum.28 = f32[16,16]{0,1:T(8,128)S(1)} all-reduce(f32[16,16]{0,1:T(8,128)S(1)} %fusion.22), channel_id=1, replica_groups=mesh['rep'=16,'shard'=32] {'shard'}, use_global_device_ids=true, to_apply=%region_0.1 | all-reduce | flops 256 | bytes 2048 | tf_op jit(solution)/shard_map/psum | solution.py:35
  94.3 0.1 copy.5
  94.4 1.5 cholesky.44
  95.8 0.6 compare_reduce_fusion.1
  96.5 0.6 fusion.12
  97.2 1.2 custom-call.6
  98.4 0.2 fusion.17
  98.6 0.0 copy-done
  98.6 1.0 convolution_multiply_fusion.3
  99.6 0.0 all-reduce.3.cloned.1.call-update
  99.6 0.0 all-reduce.5.cloned.1.call-start
  99.7 150.5 %all-reduce.3.cloned.1.call-done = f32[16,5120]{1,0:T(8,128)} async-done(((f32[16,5120]{1,0:T(8,128)}), f32[16,5120]{1,0:T(8,128)}) %all-reduce.3.cloned.1.call-update) | async-done | bytes 327696 | tf_op jit(solution)/shard_map/psum | solution.py:41
  250.2 1.9 collective-permute-start.1
  252.1 0.0 copy-start.3
  252.1 1.8 collective-permute-done.1
  253.9 3.3 fusion.1
  257.3 0.0 copy-done.3
  257.3 0.4 convolution_bitcast_fusion
  257.7 0.0 copy-start.1
  257.7 5.7 %collective-permute-start.2 = (f32[16,128]{1,0:T(8,128)S(1)}, f32[16,128]{1,0:T(8,128)S(1)}, u32[]{:S(2)}, u32[]{:S(2)}) collective-permute-start(f32[16,128]{1,0:T(8,128)S(1)} %convolution_bitcast_fusion), channel_id=1, source_target_pairs={{0,256},{32,288},{64,320},{96,352},{128,384},{160,416},{192,448},{... | collective-permute-start | bytes 24584 | tf_op jit(solution)/shard_map/ppermute | solution.py:10
  263.4 3.9 collective-permute-done.2
  267.3 0.1 fusion.23
  267.5 72.9 %psum.30 = f32[16,16]{0,1:T(8,128)S(1)} all-reduce(f32[16,16]{0,1:T(8,128)S(1)} %fusion.23), channel_id=1, replica_groups=mesh['rep'=16,'shard'=32] {'shard'}, use_global_device_ids=true, to_apply=%region_4.7 | all-reduce | flops 256 | bytes 2048 | tf_op jit(solution)/shard_map/psum | solution.py:35
  340.3 0.1 copy.7
  340.4 1.5 cholesky.55
  341.9 0.6 compare_reduce_fusion
  342.6 0.6 fusion.13
  343.2 1.2 custom-call.7
  344.4 0.2 fusion.14
  344.6 1.0 convolution_multiply_fusion.2
  345.7 0.0 all-reduce.5.cloned.1.call-update
  345.7 150.4 %all-reduce.5.cloned.1.call-done = f32[16,5120]{1,0:T(8,128)} async-done(((f32[16,5120]{1,0:T(8,128)}), f32[16,5120]{1,0:T(8,128)}) %all-reduce.5.cloned.1.call-update) | async-done | bytes 327696 | tf_op jit(solution)/shard_map/psum | solution.py:41
  496.1 5.6 %collective-permute-start.3 = (f32[16,5120]{1,0:T(8,128)}, f32[16,5120]{1,0:T(8,128)S(1)}, u32[]{:S(2)}, u32[]{:S(2)}) collective-permute-start(f32[16,5120]{1,0:T(8,128)} %all-reduce.5.cloned.1.call-done), channel_id=1, source_target_pairs={{0,256},{32,288},{64,320},{96,352},{128,384},{160,416},{192,448},{... | collective-permute-start | bytes 983048 | tf_op jit(solution)/shard_map/ppermute | solution.py:10
  501.7 0.0 copy-done.1
  501.8 0.0 copy-start.2
  501.8 11.9 %collective-permute-done.3 = f32[16,5120]{1,0:T(8,128)S(1)} collective-permute-done((f32[16,5120]{1,0:T(8,128)}, f32[16,5120]{1,0:T(8,128)S(1)}, u32[]{:S(2)}, u32[]{:S(2)}) %collective-permute-start.3) | collective-permute-done | bytes 327712 | tf_op jit(solution)/shard_map/ppermute | solution.py:10
  513.6 1.0 add_bitcast_fusion
  514.6 0.9 maximum_bitcast_fusion
  515.5 0.0 copy-done.2
  515.5 3.4 fusion.2
  (5 shorter events, 0.1 us)
Async XLA Ops:
  7.2 91.4 %copy-start = (bf16[1,128,5120]{2,1,0:T(8,128)(2,1)S(1)}, bf16[1,128,5120]{2,1,0:T(8,128)(2,1)}, u32[]{:S(2)}) copy-start(bf16[1,128,5120]{2,1,0:T(8,128)(2,1)} %param.5) | copy-start | bytes 3932164
  7.2 243.0 %all-reduce.3.cloned.1.call-start = ((), (), s32[]{:S(2)}) async-start(), calls=%async_computation | async-start | bytes 655360 | tf_op jit(solution)/shard_map/psum | solution.py:41
  9.1 3.1 collective-permute-start
  99.6 396.5 %all-reduce.5.cloned.1.call-start = ((), (), s32[]{:S(2)}) async-start(), calls=%async_computation.1 | async-start | bytes 655360 | tf_op jit(solution)/shard_map/psum | solution.py:41
  250.2 3.7 collective-permute-start.1
  252.1 5.2 copy-start.3
  257.7 244.0 %copy-start.1 = (f32[16,5120]{1,0:T(8,128)S(1)}, f32[16,5120]{1,0:T(8,128)}, u32[]{:S(2)}) copy-start(f32[16,5120]{1,0:T(8,128)} %all-reduce.3.cloned.1.call-done) | copy-start | bytes 983044
  257.7 9.6 %collective-permute-start.2 = (f32[16,128]{1,0:T(8,128)S(1)}, f32[16,128]{1,0:T(8,128)S(1)}, u32[]{:S(2)}, u32[]{:S(2)}) collective-permute-start(f32[16,128]{1,0:T(8,128)S(1)} %convolution_bitcast_fusion), channel_id=1, source_target_pairs={{0,256},{32,288},{64,320},{96,352},{128,384},{160,416},{192,448},{... | collective-permute-start | bytes 24584 | tf_op jit(solution)/shard_map/ppermute | solution.py:10
  496.1 17.5 %collective-permute-start.3 = (f32[16,5120]{1,0:T(8,128)}, f32[16,5120]{1,0:T(8,128)S(1)}, u32[]{:S(2)}, u32[]{:S(2)}) collective-permute-start(f32[16,5120]{1,0:T(8,128)} %all-reduce.5.cloned.1.call-done), channel_id=1, source_target_pairs={{0,256},{32,288},{64,320},{96,352},{128,384},{160,416},{192,448},{... | collective-permute-start | bytes 983048 | tf_op jit(solution)/shard_map/ppermute | solution.py:10
  501.8 13.8 %copy-start.2 = (f32[16,5120]{1,0:T(8,128)S(1)}, f32[16,5120]{1,0:T(8,128)}, u32[]{:S(2)}) copy-start(f32[16,5120]{1,0:T(8,128)} %all-reduce.5.cloned.1.call-done) | copy-start | bytes 983044
Sparse Core Ops, SparseCore 0:
  99.8 150.3 all-reduce.2
  345.8 150.2 all-reduce.4
where the time goes:
time: 526 us
  waiting for transfers between devices  320 us (61%)
  blocking collectives  155 us (29%)
  starting transfers between devices  15.2 us (3%)
  between operations  14.2 us (3%)
  matrix products  11.8 us (2%)
  other arithmetic  9.95 us (2%)
    psum x2, waiting for transfers between devices, shards(): summed = lax.psum(signed, 'shard')  301 us
    psum x2, blocking collectives, shards(): gram_sum = lax.psum(gram_local, 'shard')  155 us
    ppermute x4, waiting for transfers between devices, partner(): lax.ppermute(value, axis, [(i, i ^ 1 << stride) for i in range(lax.axis_s...  18.7 us
    ppermute x4, starting transfers between devices, partner(): lax.ppermute(value, axis, [(i, i ^ 1 << stride) for i in range(lax.axis_s...  15.1 us
  transfers between devices with their start and end apart: 6, of which 6 were waited for; matrix products, arithmetic and copies ran while one was open for 0% of the time, Pallas kernels for 0%

commit v1 on v0

v1 whole, which is shorter than its diff:
```python
import functools

import jax
import jax.numpy as jnp
from jax import lax
from jax.experimental import pallas as pl
from jax.experimental.pallas import tpu as pltpu
from jax.sharding import Mesh
from jax.sharding import PartitionSpec as P

RANK = 16
LANES = 128
NX, NZ = 4, 8
TILES = 10
GROUP = 32
HIGHEST = lax.Precision.HIGHEST
F32 = jnp.float32
BF16 = jnp.bfloat16
VMEM = pl.BlockSpec(memory_space=pltpu.VMEM)


def call(body, out, ins, flops=1_000_000, data=1_000_000):
    return pl.pallas_call(
        body,
        out_shape=out,
        in_specs=[VMEM] * ins,
        out_specs=jax.tree.map(lambda _: VMEM, out),
        compiler_params=pltpu.CompilerParams(vmem_limit_bytes=40 * 2**20),
        cost_estimate=pl.CostEstimate(flops=flops, bytes_accessed=data, transcendentals=0),
    )


def shape(*dims, dtype=F32):
    return jax.ShapeDtypeStruct(dims, dtype)


def dot(a, b, precision=HIGHEST):
    return jnp.dot(a, b, precision=precision, preferred_element_type=F32)


def dot_t(a, b, precision=HIGHEST):
    return lax.dot_general(
        a, b, (((1,), (1,)), ((), ())), precision=precision, preferred_element_type=F32
    )


def pieces(value):
    high = value.astype(BF16)
    return high, (value - high.astype(F32)).astype(BF16)


def signs():
    even = (1 - 2 * lax.axis_index("c")).astype(F32)
    low = (1 - 2 * lax.axis_index("h")).astype(F32)
    return even, low


def sketch_body(sketch_ref, starts_ref, weight_ref, send_ref):
    crossed = lax.dot_general(
        starts_ref[...].astype(BF16),
        weight_ref[...],
        (((1,), (1,)), ((), ())),
        preferred_element_type=F32,
    )
    for n in range(4):
        send_ref[n, 0:32, :] = sketch_ref[...]
        send_ref[n, 32:48, :] = crossed


def project_body(sketch_ref, weight_ref, send_ref, stack_ref):
    half, core = lax.axis_index("h"), lax.axis_index("c")
    even, low = signs()
    mine = sketch_ref[2 * half + core]
    side = sketch_ref[2 * half + 1 - core]
    far = sketch_ref[2 * (1 - half) + core]
    far_side = sketch_ref[2 * (1 - half) + 1 - core]
    cross = low * (mine[16:32] - far[16:32])
    own = even * (mine[0:16] - side[0:16])
    other = even * (far[0:16] - far_side[0:16])
    start_own = even * (mine[16:32] - side[32:48])
    start_other = even * (far[16:32] - far_side[32:48])
    stack = jnp.concatenate([cross, own, other], axis=0)
    stack_ref[...] = stack
    zero = jnp.zeros((RANK, LANES), F32)

    def gram_rows(left, right):
        return dot_t(left, jnp.concatenate(right, axis=0))

    gram = (
        gram_rows(cross, [cross, own, other] + [zero] * 5)
        + gram_rows(own, [zero] * 3 + [own, other, start_own] + [zero] * 2)
        + gram_rows(other, [zero] * 6 + [other, start_other])
    )
    high, low_part = pieces(stack)
    both = jnp.concatenate([high, low_part], axis=0)
    for x in range(NX):
        span = TILES * LANES
        product = jnp.dot(
            both, weight_ref[:, x * span : (x + 1) * span], preferred_element_type=F32
        )
        product = product[0:48] + product[48:96]
        for t in range(TILES):
            send_ref[x, t * 48 : (t + 1) * 48, :] = product[:, t * LANES : (t + 1) * LANES]
        send_ref[x, TILES * 48 : TILES * 48 + 16, :] = gram


def lane_group():
    return lax.broadcasted_iota(jnp.int32, (RANK, LANES), 1) // GROUP


def first_sum_body(got_ref, send_ref):
    def total(start, size):
        rows = pl.ds(start, size)
        return (got_ref[0, rows, :] + got_ref[1, rows, :]) + (
            got_ref[2, rows, :] + got_ref[3, rows, :]
        )

    gram = total(TILES * 48, 16)
    lanes = lane_group()
    rests = [total((NZ + k) * 48, 48) for k in range(2)]
    for z in range(NZ):
        send_ref[z, 0:48, :] = total(z * 48, 48)
        k, g = z // 4, z % 4
        packed = jnp.zeros((RANK, LANES), F32)
        for a in range(3):
            piece = rests[k][16 * a : 16 * a + 16]
            shift = (GROUP * (a - g)) % LANES
            if shift:
                piece = pltpu.roll(piece, shift, 1)
            packed = jnp.where(lanes == a, piece, packed)
        send_ref[z, 48:64, :] = packed
        send_ref[z, 64:80, :] = gram


def second_sum_body(got_ref, sums_ref, side_ref, gram_ref):
    total = got_ref[0]
    for z in range(1, NZ):
        total = total + got_ref[z]
    sums_ref[...] = total[0:64]
    side_ref[0:16, :] = total[16:32]
    side_ref[16:32, :] = total[48:64]
    gram_ref[...] = total[64:80]


def eye():
    rows = lax.broadcasted_iota(jnp.int32, (RANK, RANK), 0)
    cols = lax.broadcasted_iota(jnp.int32, (RANK, RANK), 1)
    return rows, (rows == cols).astype(F32)


def inverse_factors(grams):
    rows, unit = eye()
    left = list(grams)
    right = [unit] * len(grams)
    for j in range(RANK - 1):
        for i in range(len(grams)):
            ratio = left[i][:, j : j + 1] / left[i][j : j + 1, j : j + 1]
            ratio = jnp.where(rows > j, ratio, 0.0)
            left[i] = left[i] - ratio * left[i][j : j + 1, :]
            right[i] = right[i] - ratio * right[i][j : j + 1, :]
    out = []
    for i in range(len(grams)):
        pivots = jnp.sum(left[i] * unit, axis=1, keepdims=True)
        out.append(right[i] * lax.rsqrt(pivots))
    return out


def factor_body(gram_ref, stack_ref, mix_ref, basis_ref):
    even, low = signs()
    scale = -0.5 * low * even
    blocks = [gram_ref[:, 16 * b : 16 * b + 16] for b in range(8)]
    b0, b1, b2, b3, b4, b5, b6, b7 = blocks
    inv_own, inv_other = inverse_factors([b3, b6])
    gamma_own = dot(inv_own.T, inv_own)
    gamma_other = dot(inv_other.T, inv_other)
    q_own, q_other = b5.T, b7.T
    m_own = scale * dot(q_own, gamma_own)
    m_other = -scale * dot(q_other, gamma_other)
    kg0 = b0 + dot_t(m_own, b1) + dot_t(m_other, b2)
    kg1 = b1 + scale * q_own + dot_t(m_other, b4)
    kg2 = b2 + dot(m_own, b4) - scale * q_other
    gram1 = kg0 + dot_t(kg1, m_own) + dot_t(kg2, m_other)
    (inv1,) = inverse_factors([gram1])
    c_own = scale * even * dot(inv1, dot(kg1, gamma_own))
    c_other = -scale * even * dot(inv1, dot(kg2, gamma_other))
    n_own = dot(inv1, m_own)
    n_other = dot(inv1, m_other)
    zero = jnp.zeros((RANK, RANK), F32)
    first = [zero, even * inv_own, zero, -even * inv_own, zero, zero, zero, zero]
    second = [
        low * inv1,
        low * n_own + c_own,
        low * n_other,
        -c_own,
        -low * inv1,
        c_other - low * n_other,
        -low * n_own,
        -c_other,
    ]
    for b in range(8):
        mix_ref[0:16, 16 * b : 16 * b + 16] = first[b]
        mix_ref[16:32, 16 * b : 16 * b + 16] = second[b]
    cross, own, other = stack_ref[0:16], stack_ref[16:32], stack_ref[32:48]
    basis0 = (0.5 * even) * dot(inv_own, own)
    basis1 = (0.5 * low) * (dot(inv1, cross) + dot(n_own, own) + dot(n_other, other))
    basis_ref[...] = jnp.concatenate([basis0, basis1], axis=0)


def combine_body(sums_ref, side_ref, far_ref, far_side_ref, mix_ref, send_ref):
    rest, far_rest = sums_ref[48:64], far_ref[48:64]
    side_rest, far_side_rest = side_ref[16:32], far_side_ref[16:32]

    def turned(value, a):
        return pltpu.roll(value, LANES - GROUP * a, 1) if a else value

    main = jnp.concatenate(
        [sums_ref[0:48], side_ref[0:16], far_ref[0:48], far_side_ref[0:16]], axis=0
    )
    tail = jnp.concatenate(
        [turned(rest, a) for a in range(3)]
        + [turned(side_rest, 1)]
        + [turned(far_rest, a) for a in range(3)]
        + [turned(far_side_rest, 1)],
        axis=0,
    )
    mix = mix_ref[...]
    head = dot(mix, main)
    tail = dot(mix, tail)
    lanes = lane_group()[0:8]
    packed = tail[0:8]
    for a in range(1, 4):
        packed = jnp.where(lanes == a, pltpu.roll(tail[8 * a : 8 * a + 8], GROUP * a, 1), packed)
    for n in range(NX * NZ):
        send_ref[n, 0:32, :] = head
        send_ref[n, 32:40, :] = packed


def update_body(got_ref, weight_ref, basis_ref, corrected_ref, factors_ref):
    lanes = lane_group()[0:8]
    tiles = [got_ref[z, 0:32, :] for z in range(NZ)]
    for k in range(2):
        groups = []
        for a in range(4):
            row = None
            for g in range(4):
                piece = got_ref[4 * k + g, 32:40, :]
                shift = (GROUP * (g - a)) % LANES
                if shift:
                    piece = pltpu.roll(piece, shift, 1)
                row = piece if row is None else jnp.where(lanes == g, piece, row)
            groups.append(row)
        tiles.append(jnp.concatenate(groups, axis=0))
    transposed = basis_ref[...].T
    columns = []
    for k in range(2):
        high, low = pieces(transposed[:, 16 * k : 16 * k + 16])
        columns.append(jnp.concatenate([high, low, high], axis=1))
    for t in range(TILES):
        span = pl.ds(t * LANES, LANES)
        current = weight_ref[:, span].astype(F32)
        for k in range(2):
            factor = tiles[t][16 * k : 16 * k + 16]
            factors_ref[0, k, :, span] = factor
            high, low = pieces(factor)
            change = jnp.dot(
                columns[k], jnp.concatenate([high, high, low], axis=0), preferred_element_type=F32
            )
            rounded = (current - change).astype(BF16)
            current = rounded.astype(F32)
        corrected_ref[:, span] = rounded


def flip(value, axis):
    return lax.ppermute(value, axis, [(0, 1), (1, 0)])


def flip_both(value):
    return lax.ppermute(value, ("h", "c"), [(0, 3), (1, 2), (2, 1), (3, 0)])


def shards(weights, warm_start):
    weight = weights[0]
    starts = warm_start[0]
    rows, cols = weight.shape
    swapped = flip(starts[1].astype(F32), "c")
    sketch = lax.dot_general(
        starts.reshape(2 * RANK, cols),
        weight,
        (((1,), (1,)), ((), ())),
        preferred_element_type=F32,
    )
    sketch = call(sketch_body, shape(4, 48, rows), 3)(sketch, swapped, weight)
    sketch = lax.all_to_all(sketch, ("h", "c"), 0, 0)
    depth = TILES * 48 + 16
    send, stack = call(
        project_body, (shape(NX, depth, LANES), shape(48, LANES)), 2, 130_000_000, 4_000_000
    )(sketch, weight)
    got = lax.all_to_all(send, "x", 0, 0)
    send = call(first_sum_body, shape(NZ, 80, LANES), 1)(got)
    got = lax.all_to_all(send, "z", 0, 0)
    sums, side, gram = call(
        second_sum_body, (shape(64, LANES), shape(32, LANES), shape(16, LANES)), 1
    )(got)
    far = flip(sums, "h")
    near_side = flip(side, "c")
    far_side = flip_both(side)
    mix, basis = call(
        factor_body, (shape(32, LANES), shape(32, LANES)), 2, 500_000_000, 10_000_000
    )(gram, stack)
    send = call(combine_body, shape(NX * NZ, 40, LANES), 5)(sums, near_side, far, far_side, mix)
    got = lax.all_to_all(send, ("x", "z"), 0, 0)
    span = TILES * LANES
    corrected, factors = pl.pallas_call(
        update_body,
        grid=(NX,),
        out_shape=(shape(rows, cols, dtype=BF16), shape(1, 2, RANK, cols)),
        in_specs=[
            pl.BlockSpec((NZ, 40, LANES), lambda i: (i, 0, 0)),
            pl.BlockSpec((rows, span), lambda i: (0, i)),
            pl.BlockSpec((32, LANES), lambda i: (0, 0)),
        ],
        out_specs=(
            pl.BlockSpec((rows, span), lambda i: (0, i)),
            pl.BlockSpec((1, 2, RANK, span), lambda i: (0, 0, 0, i)),
        ),
        compiler_params=pltpu.CompilerParams(vmem_limit_bytes=40 * 2**20),
    )(got, weight, basis)
    return corrected[None], factors


def solution(mesh):
    inner = Mesh(mesh.devices.reshape(2, 4, 2, NX, NZ), ("h", "y", "c", "x", "z"))
    placed = (P(("h", "y", "c"), ("x", "z"), None), P(("h", "y", "c"), None, None, None))
    return jax.shard_map(
        shards, mesh=inner, in_specs=placed, out_specs=placed, check_vma=False
    )
```

time: 526 us -> 105 us (0.20)
  the two profiles are of different devices: /device:TPU:16 before, /device:TPU:8 now
where the time goes in v1:
time: 105 us
  blocking collectives  78.8 us (75%)
  starting transfers between devices  13.7 us (13%)
  Pallas kernels  8.49 us (8%)
  matrix products  1.95 us (2%)
    all_to_all x1, blocking collectives, shards(): got = lax.all_to_all(send, ('x', 'z'), 0, 0)  23.3 us
    all_to_all x1, blocking collectives, shards(): got = lax.all_to_all(send, 'z', 0, 0)  21.6 us
    all_to_all x1, blocking collectives, shards(): got = lax.all_to_all(send, 'x', 0, 0)  18.6 us
    all_to_all x1, blocking collectives, shards(): sketch = lax.all_to_all(sketch, ('h', 'c'), 0, 0)  15.4 us
    ppermute x3, starting transfers between devices, flip(): return lax.ppermute(value, axis, [(0, 1), (1, 0)])  11.8 us
    pallas_call x1, Pallas kernels, shards(): call(factor_body, (shape(32, LANES), shape(32, LANES)), 2, 500000000, 100...  3.97 us
    pallas_call x1, Pallas kernels, shards(): pl.pallas_call(update_body, grid=(NX,), out_shape=(shape(rows, cols, dtyp...  2.99 us
  transfers between devices with their start and end apart: 4, of which 0 were waited for; matrix products, arithmetic and copies ran while one was open for 2% of the time, Pallas kernels for 4%

profile of v1, /device:TPU:8, one launch (start us, length us, event | category | flops | bytes accessed | tf_op | source)
XLA Modules:
  0.0 104.8 jit_solution(2408490081565434472)
XLA Ops:
  0.6 0.0 copy-start
  0.6 1.0 bitcast_convert_fusion
  1.7 1.9 %collective-permute-start = (f32[16,5120]{1,0:T(8,128)S(1)}, f32[16,5120]{1,0:T(8,128)S(1)}, u32[]{:S(2)}, u32[]{:S(2)}) collective-permute-start(f32[16,5120]{1,0:T(8,128)S(1)} %bitcast_convert_fusion), channel_id=1, source_target_pairs={{0,32},{32,0},{1,33},{33,1},{2,34},{34,2},{3,35},{35,3},{4,36},{36... | collective-permute-start | bytes 983048 | tf_op jit(solution)/shard_map/ppermute | solution.py:274
  3.6 2.0 %fusion.sketch_ref = f32[32,128]{1,0:T(8,128)S(1)} fusion(bf16[32,5120]{1,0:T(8,128)(2,1)} %bitcast.12, bf16[1,128,5120]{2,1,0:T(8,128)(2,1)} %param.2), kind=kOutput, calls=%fused_computation.1 | convolution fusion | flops 41943040 | bytes 1654784 | tf_op jit(solution)/shard_map/dot_general | solution.py:286
  5.6 0.0 collective-permute-done.starts_ref
  5.6 0.0 copy-done
  5.6 0.4 shard_map.41
  6.0 15.4 %all_to_all.20.sketch_ref = f32[4,48,128]{2,1,0:T(8,128)S(1)} all-to-all(f32[4,48,128]{2,1,0:T(8,128)S(1)} %shard_map.41), channel_id=1, replica_groups=mesh['h'=2,'y'=4,'c'=2,'x'=4,'z'=8] {'h','c'}, dimensions={0} | all-to-all | bytes 196608 | tf_op jit(solution)/shard_map/all_to_all | solution.py:293
  21.4 0.6 shard_map.42
  22.0 18.6 %all_to_all.21.got_ref = f32[4,496,128]{2,1,0:T(8,128)S(1)} all-to-all(f32[4,496,128]{2,1,0:T(8,128)S(1)} %get-tuple-element.11), channel_id=1, replica_groups=mesh['h'=2,'y'=4,'c'=2,'x'=4,'z'=8] {'x'}, dimensions={0} | all-to-all | bytes 2031616 | tf_op jit(solution)/shard_map/all_to_all | solution.py:298
  40.6 0.1 shard_map.43
  40.7 21.6 %all_to_all.22.got_ref = f32[8,80,128]{2,1,0:T(8,128)S(1)} all-to-all(f32[8,80,128]{2,1,0:T(8,128)S(1)} %shard_map.43), channel_id=1, replica_groups=mesh['h'=2,'y'=4,'c'=2,'x'=4,'z'=8] {'z'}, dimensions={0} | all-to-all | bytes 655360 | tf_op jit(solution)/shard_map/all_to_all | solution.py:300
  62.3 1.9 %collective-permute-start.3 = (f32[32,128]{1,0:T(8,128)S(1)}, f32[32,128]{1,0:T(8,128)S(1)}, u32[]{:S(2)}, u32[]{:S(2)}) collective-permute-start(f32[32,128]{1,0:T(8,128)S(1)} %get-tuple-element.13), channel_id=1, source_target_pairs={{0,288},{32,256},{256,32},{288,0},{1,289},{33,257},{257,33},{289,1... | collective-permute-start | bytes 49160 | tf_op jit(solution)/shard_map/ppermute | solution.py:278
  64.2 3.3 %collective-permute-start.1 = (f32[32,128]{1,0:T(8,128)S(1)}, f32[32,128]{1,0:T(8,128)S(1)}, u32[]{:S(2)}, u32[]{:S(2)}) collective-permute-start(f32[32,128]{1,0:T(8,128)S(1)} %get-tuple-element.13), channel_id=1, source_target_pairs={{0,32},{32,0},{1,33},{33,1},{2,34},{34,2},{3,35},{35,3},{4,36},{36... | collective-permute-start | bytes 49160 | tf_op jit(solution)/shard_map/ppermute | solution.py:274
  67.6 6.5 %collective-permute-start.2 = (f32[64,128]{1,0:T(8,128)S(1)}, f32[64,128]{1,0:T(8,128)S(1)}, u32[]{:S(2)}, u32[]{:S(2)}) collective-permute-start(f32[64,128]{1,0:T(8,128)S(1)} %get-tuple-element.12.sums_ref), channel_id=1, source_target_pairs={{0,256},{256,0},{1,257},{257,1},{2,258},{258,2},{3,259},{259,3},{4... | collective-permute-start | bytes 98312 | tf_op jit(solution)/shard_map/ppermute | solution.py:274
  74.1 4.0 %shard_map.45 = (f32[32,128]{1,0:T(8,128)S(1)}, f32[32,128]{1,0:T(8,128)S(1)}) custom-call(f32[16,128]{1,0:T(8,128)S(1)} %get-tuple-element.14.gram_ref, f32[48,128]{1,0:T(8,128)S(1)} %get-tuple-element.15.stack_ref), custom_call_target="tpu_custom_call" | custom-call | flops 500000000 | bytes 10000000 | tf_op jit(solution)/shard_map/pallas_call | solution.py:307
  78.1 0.0 collective-permute-done.3.far_side_ref
  78.1 0.0 collective-permute-done.1.side_ref
  78.1 0.0 collective-permute-done.2.far_ref
  78.1 0.4 shard_map.46
  78.5 23.3 %all_to_all.23.got_ref = f32[32,40,128]{2,1,0:T(8,128)S(1)} all-to-all(f32[32,40,128]{2,1,0:T(8,128)S(1)} %shard_map.46), channel_id=1, replica_groups=mesh['h'=2,'y'=4,'c'=2,'x'=4,'z'=8] {'x','z'}, dimensions={0} | all-to-all | bytes 1310720 | tf_op jit(solution)/shard_map/all_to_all | solution.py:311
  101.8 3.0 %shard_map.47 = (bf16[128,5120]{1,0:T(8,128)(2,1)}, f32[1,2,16,5120]{3,2,1,0:T(8,128)}) custom-call(f32[32,40,128]{2,1,0:T(8,128)S(1)} %all_to_all.23.got_ref, bf16[128,5120]{1,0:T(8,128)(2,1)S(1)} %bitcast.11, f32[32,128]{1,0:T(8,128)S(1)} %get-tuple-element.17.basis_ref), custom_call_target="tpu_custom_call" | custom-call | tf_op jit(solution)/shard_map/pallas_call | solution.py:313
  (1 shorter events, 0.0 us)
Async XLA Ops:
  0.6 5.0 %copy-start = (bf16[1,128,5120]{2,1,0:T(8,128)(2,1)S(1)}, bf16[1,128,5120]{2,1,0:T(8,128)(2,1)}, u32[]{:S(2)}) copy-start(bf16[1,128,5120]{2,1,0:T(8,128)(2,1)} %param.2) | copy-start | bytes 3932164
  1.7 3.9 %collective-permute-start = (f32[16,5120]{1,0:T(8,128)S(1)}, f32[16,5120]{1,0:T(8,128)S(1)}, u32[]{:S(2)}, u32[]{:S(2)}) collective-permute-start(f32[16,5120]{1,0:T(8,128)S(1)} %bitcast_convert_fusion), channel_id=1, source_target_pairs={{0,32},{32,0},{1,33},{33,1},{2,34},{34,2},{3,35},{35,3},{4,36},{36... | collective-permute-start | bytes 983048 | tf_op jit(solution)/shard_map/ppermute | solution.py:274
  62.3 15.8 %collective-permute-start.3 = (f32[32,128]{1,0:T(8,128)S(1)}, f32[32,128]{1,0:T(8,128)S(1)}, u32[]{:S(2)}, u32[]{:S(2)}) collective-permute-start(f32[32,128]{1,0:T(8,128)S(1)} %get-tuple-element.13), channel_id=1, source_target_pairs={{0,288},{32,256},{256,32},{288,0},{1,289},{33,257},{257,33},{289,1... | collective-permute-start | bytes 49160 | tf_op jit(solution)/shard_map/ppermute | solution.py:278
  64.2 13.8 %collective-permute-start.1 = (f32[32,128]{1,0:T(8,128)S(1)}, f32[32,128]{1,0:T(8,128)S(1)}, u32[]{:S(2)}, u32[]{:S(2)}) collective-permute-start(f32[32,128]{1,0:T(8,128)S(1)} %get-tuple-element.13), channel_id=1, source_target_pairs={{0,32},{32,0},{1,33},{33,1},{2,34},{34,2},{3,35},{35,3},{4,36},{36... | collective-permute-start | bytes 49160 | tf_op jit(solution)/shard_map/ppermute | solution.py:274
  67.6 10.5 %collective-permute-start.2 = (f32[64,128]{1,0:T(8,128)S(1)}, f32[64,128]{1,0:T(8,128)S(1)}, u32[]{:S(2)}, u32[]{:S(2)}) collective-permute-start(f32[64,128]{1,0:T(8,128)S(1)} %get-tuple-element.12.sums_ref), channel_id=1, source_target_pairs={{0,256},{256,0},{1,257},{257,1},{2,258},{258,2},{3,259},{259,3},{4... | collective-permute-start | bytes 98312 | tf_op jit(solution)/shard_map/ppermute | solution.py:274

commit v2 on v1

--- a/solution.py
+++ b/solution.py
@@ -132,13 +132,12 @@
         send_ref[z, 64:80, :] = gram
 
 
-def second_sum_body(got_ref, sums_ref, side_ref, gram_ref):
+def second_sum_body(got_ref, send_ref, gram_ref):
     total = got_ref[0]
     for z in range(1, NZ):
         total = total + got_ref[z]
-    sums_ref[...] = total[0:64]
-    side_ref[0:16, :] = total[16:32]
-    side_ref[16:32, :] = total[48:64]
+    for n in range(4):
+        send_ref[n] = total[0:64]
     gram_ref[...] = total[64:80]
 
 
@@ -206,15 +205,24 @@
     basis_ref[...] = jnp.concatenate([basis0, basis1], axis=0)
 
 
-def combine_body(sums_ref, side_ref, far_ref, far_side_ref, mix_ref, send_ref):
-    rest, far_rest = sums_ref[48:64], far_ref[48:64]
-    side_rest, far_side_rest = side_ref[16:32], far_side_ref[16:32]
+def combine_body(sums_ref, mix_ref, send_ref):
+    half, core = lax.axis_index("h"), lax.axis_index("c")
+    mine, side = 2 * half + core, 2 * half + 1 - core
+    far, far_side = 2 * (1 - half) + core, 2 * (1 - half) + 1 - core
+    rest, far_rest = sums_ref[mine, 48:64, :], sums_ref[far, 48:64, :]
+    side_rest, far_side_rest = sums_ref[side, 48:64, :], sums_ref[far_side, 48:64, :]
 
     def turned(value, a):
         return pltpu.roll(value, LANES - GROUP * a, 1) if a else value
 
     main = jnp.concatenate(
-        [sums_ref[0:48], side_ref[0:16], far_ref[0:48], far_side_ref[0:16]], axis=0
+        [
+            sums_ref[mine, 0:48, :],
+            sums_ref[side, 16:32, :],
+            sums_ref[far, 0:48, :],
+            sums_ref[far_side, 16:32, :],
+        ],
+        axis=0,
     )
     tail = jnp.concatenate(
         [turned(rest, a) for a in range(3)]
@@ -235,47 +243,58 @@
         send_ref[n, 32:40, :] = packed
 
 
-def update_body(got_ref, weight_ref, basis_ref, corrected_ref, factors_ref):
+def update_body(
+    got_ref, weight_ref, basis_ref, corrected_hbm, factors_hbm, corrected_ref, factors_ref, sems
+):
     lanes = lane_group()[0:8]
-    tiles = [got_ref[z, 0:32, :] for z in range(NZ)]
-    for k in range(2):
-        groups = []
-        for a in range(4):
-            row = None
-            for g in range(4):
-                piece = got_ref[4 * k + g, 32:40, :]
-                shift = (GROUP * (g - a)) % LANES
-                if shift:
-                    piece = pltpu.roll(piece, shift, 1)
-                row = piece if row is None else jnp.where(lanes == g, piece, row)
-            groups.append(row)
-        tiles.append(jnp.concatenate(groups, axis=0))
+    span = TILES * LANES
     transposed = basis_ref[...].T
-    columns = []
+    left = []
     for k in range(2):
         high, low = pieces(transposed[:, 16 * k : 16 * k + 16])
-        columns.append(jnp.concatenate([high, low, high], axis=1))
-    for t in range(TILES):
-        span = pl.ds(t * LANES, LANES)
-        current = weight_ref[:, span].astype(F32)
+        left.append(jnp.concatenate([high, low, high], axis=1))
+    copies = []
+    for x in range(NX):
+        tiles = [got_ref[x * NZ + z, 0:32, :] for z in range(NZ)]
         for k in range(2):
-            factor = tiles[t][16 * k : 16 * k + 16]
-            factors_ref[0, k, :, span] = factor
-            high, low = pieces(factor)
-            change = jnp.dot(
-                columns[k], jnp.concatenate([high, high, low], axis=0), preferred_element_type=F32
-            )
-            rounded = (current - change).astype(BF16)
-            current = rounded.astype(F32)
-        corrected_ref[:, span] = rounded
+            groups = []
+            for a in range(4):
+                row = None
+                for g in range(4):
+                    piece = got_ref[x * NZ + 4 * k + g, 32:40, :]
+                    shift = (GROUP * (g - a)) % LANES
+                    if shift:
+                        piece = pltpu.roll(piece, shift, 1)
+                    row = piece if row is None else jnp.where(lanes == g, piece, row)
+                groups.append(row)
+            tiles.append(jnp.concatenate(groups, axis=0))
+        for t in range(0, TILES, 2):
+            part = pl.ds(x * span + t * LANES, 2 * LANES)
+            pair = jnp.concatenate(tiles[t : t + 2], axis=1)
+            current = weight_ref[:, part].astype(F32)
+            for k in range(2):
+                factor = pair[16 * k : 16 * k + 16]
+                factors_ref[k, :, part] = factor
+                high, low = pieces(factor)
+                right = jnp.concatenate([high, high, low], axis=0)
+                change = jnp.dot(left[k], right, preferred_element_type=F32)
+                rounded = (current - change).astype(BF16)
+                current = rounded.astype(F32)
+            corrected_ref[:, part] = rounded
+        part = pl.ds(x * span, span)
+        for i, (source, target) in enumerate(
+            ((corrected_ref, corrected_hbm), (factors_ref, factors_hbm))
+        ):
+            index = (slice(None),) * (1 + i) + (part,)
+            copy = pltpu.make_async_copy(source.at[index], target.at[index], sems.at[2 * x + i])
+            copy.start()
+            copies.append(copy)
+    for copy in copies:
+        copy.wait()
 
 
 def flip(value, axis):
     return lax.ppermute(value, axis, [(0, 1), (1, 0)])
-
-
-def flip_both(value):
-    return lax.ppermute(value, ("h", "c"), [(0, 3), (1, 2), (2, 1), (3, 0)])
 
 
 def shards(weights, warm_start):
@@ -298,34 +317,27 @@
     got = lax.all_to_all(send, "x", 0, 0)
     send = call(first_sum_body, shape(NZ, 80, LANES), 1)(got)
     got = lax.all_to_all(send, "z", 0, 0)
-    sums, side, gram = call(
-        second_sum_body, (shape(64, LANES), shape(32, LANES), shape(16, LANES)), 1
-    )(got)
-    far = flip(sums, "h")
-    near_side = flip(side, "c")
-    far_side = flip_both(side)
+    send, gram = call(second_sum_body, (shape(4, 64, LANES), shape(16, LANES)), 1)(got)
+    sums = lax.all_to_all(send, ("h", "c"), 0, 0)
     mix, basis = call(
         factor_body, (shape(32, LANES), shape(32, LANES)), 2, 500_000_000, 10_000_000
     )(gram, stack)
-    send = call(combine_body, shape(NX * NZ, 40, LANES), 5)(sums, near_side, far, far_side, mix)
+    send = call(combine_body, shape(NX * NZ, 40, LANES), 2)(sums, mix)
     got = lax.all_to_all(send, ("x", "z"), 0, 0)
-    span = TILES * LANES
+    hbm = pl.BlockSpec(memory_space=pltpu.HBM)
     corrected, factors = pl.pallas_call(
         update_body,
-        grid=(NX,),
-        out_shape=(shape(rows, cols, dtype=BF16), shape(1, 2, RANK, cols)),
-        in_specs=[
-            pl.BlockSpec((NZ, 40, LANES), lambda i: (i, 0, 0)),
-            pl.BlockSpec((rows, span), lambda i: (0, i)),
-            pl.BlockSpec((32, LANES), lambda i: (0, 0)),
+        out_shape=(shape(rows, cols, dtype=BF16), shape(2, RANK, cols)),
+        in_specs=[VMEM] * 3,
+        out_specs=(hbm, hbm),
+        scratch_shapes=[
+            pltpu.VMEM((rows, cols), BF16),
+            pltpu.VMEM((2, RANK, cols), F32),
+            pltpu.SemaphoreType.DMA((2 * NX,)),
         ],
-        out_specs=(
-            pl.BlockSpec((rows, span), lambda i: (0, i)),
-            pl.BlockSpec((1, 2, RANK, span), lambda i: (0, 0, 0, i)),
-        ),
         compiler_params=pltpu.CompilerParams(vmem_limit_bytes=40 * 2**20),
     )(got, weight, basis)
-    return corrected[None], factors
+    return corrected[None], factors[None]
 
 
 def solution(mesh):

time: 105 us -> 101 us (0.962)
  starting transfers between devices: 13.7 us -> 5.25 us
  waiting for transfers between devices: 0.04 us -> 4.86 us
    ppermute x3 -> x1, starting transfers between devices: 11.8 us -> 1.92 us  [flip(): return lax.ppermute(value, axis, [(0, 1), (1, 0)])]
    all_to_all x0 -> x1, waiting for transfers between devices: none -> 4.83 us  [shards(): sums = lax.all_to_all(send, ('h', 'c'), 0, 0)]
    all_to_all x0 -> x1, starting transfers between devices: none -> 3.33 us  [shards(): sums = lax.all_to_all(send, ('h', 'c'), 0, 0)]
    ppermute x1 -> x0, starting transfers between devices: 1.92 us -> none  [flip_both(): return lax.ppermute(value, ('h', 'c'), [(0, 3), (1, 2), (2, 1), (3, 0)])]
  transfers between devices with their start and end apart: 4 -> 2, of which waited for: 0 -> 1; matrix products, arithmetic and copies ran while one was open for 2% -> 2% of each run, Pallas kernels for 4% -> 4%
where the time goes in v2:
time: 101 us
  blocking collectives  78.8 us (78%)
  Pallas kernels  7.98 us (8%)
  starting transfers between devices  5.25 us (5%)
  waiting for transfers between devices  4.86 us (5%)
  matrix products  1.95 us (2%)
  other arithmetic  1.04 us (1%)
    all_to_all x1, blocking collectives, shards(): got = lax.all_to_all(send, ('x', 'z'), 0, 0)  23.3 us
    all_to_all x1, blocking collectives, shards(): got = lax.all_to_all(send, 'z', 0, 0)  21.6 us
    all_to_all x1, blocking collectives, shards(): got = lax.all_to_all(send, 'x', 0, 0)  18.6 us
    all_to_all x1, blocking collectives, shards(): sketch = lax.all_to_all(sketch, ('h', 'c'), 0, 0)  15.4 us
    all_to_all x1, waiting for transfers between devices, shards(): sums = lax.all_to_all(send, ('h', 'c'), 0, 0)  4.83 us
    pallas_call x1, Pallas kernels, shards(): call(factor_body, (shape(32, LANES), shape(32, LANES)), 2, 500000000, 100...  3.97 us
    all_to_all x1, starting transfers between devices, shards(): sums = lax.all_to_all(send, ('h', 'c'), 0, 0)  3.33 us
  transfers between devices with their start and end apart: 2, of which 1 were waited for; matrix products, arithmetic and copies ran while one was open for 2% of the time, Pallas kernels for 4%

profile of v2, /device:TPU:8, one launch (start us, length us, event | category | flops | bytes accessed | tf_op | source)
XLA Modules:
  0.0 100.6 jit_solution(9755807409438663028)
XLA Ops:
  0.6 0.0 copy-start
  0.6 1.0 %bitcast_convert_fusion = f32[16,5120]{1,0:T(8,128)S(1)} fusion(bf16[1,2,16,5120]{3,2,1,0:T(8,128)(2,1)} %param.3), kind=kLoop, calls=%fused_computation | loop fusion | flops 81920 | bytes 491520 | tf_op jit(solution)/shard_map/convert_element_type | solution.py:304
  1.7 1.9 %collective-permute-start = (f32[16,5120]{1,0:T(8,128)S(1)}, f32[16,5120]{1,0:T(8,128)S(1)}, u32[]{:S(2)}, u32[]{:S(2)}) collective-permute-start(f32[16,5120]{1,0:T(8,128)S(1)} %bitcast_convert_fusion), channel_id=1, source_target_pairs={{0,32},{32,0},{1,33},{33,1},{2,34},{34,2},{3,35},{35,3},{4,36},{36... | collective-permute-start | bytes 983048 | tf_op jit(solution)/shard_map/ppermute | solution.py:297
  3.6 2.0 %fusion.sketch_ref = f32[32,128]{1,0:T(8,128)S(1)} fusion(bf16[32,5120]{1,0:T(8,128)(2,1)} %bitcast.13, bf16[1,128,5120]{2,1,0:T(8,128)(2,1)} %param.2), kind=kOutput, calls=%fused_computation.1 | convolution fusion | flops 41943040 | bytes 1654784 | tf_op jit(solution)/shard_map/dot_general | solution.py:305
  5.6 0.0 collective-permute-done.starts_ref
  5.6 0.0 copy-done
  5.6 0.4 shard_map.41
  6.0 15.4 %all_to_all.25.sketch_ref = f32[4,48,128]{2,1,0:T(8,128)S(1)} all-to-all(f32[4,48,128]{2,1,0:T(8,128)S(1)} %shard_map.41), channel_id=1, replica_groups=mesh['h'=2,'y'=4,'c'=2,'x'=4,'z'=8] {'h','c'}, dimensions={0} | all-to-all | bytes 196608 | tf_op jit(solution)/shard_map/all_to_all | solution.py:312
  21.4 0.6 shard_map.42
  22.0 18.6 %all_to_all.26.got_ref = f32[4,496,128]{2,1,0:T(8,128)S(1)} all-to-all(f32[4,496,128]{2,1,0:T(8,128)S(1)} %get-tuple-element.10), channel_id=1, replica_groups=mesh['h'=2,'y'=4,'c'=2,'x'=4,'z'=8] {'x'}, dimensions={0} | all-to-all | bytes 2031616 | tf_op jit(solution)/shard_map/all_to_all | solution.py:317
  40.6 0.1 shard_map.43
  40.7 21.6 %all_to_all.27.got_ref = f32[8,80,128]{2,1,0:T(8,128)S(1)} all-to-all(f32[8,80,128]{2,1,0:T(8,128)S(1)} %shard_map.43), channel_id=1, replica_groups=mesh['h'=2,'y'=4,'c'=2,'x'=4,'z'=8] {'z'}, dimensions={0} | all-to-all | bytes 655360 | tf_op jit(solution)/shard_map/all_to_all | solution.py:319
  62.3 0.7 shard_map.44
  63.0 3.3 %all-to-all-start.3 = ((f32[4,64,128]{2,1,0:T(8,128)}), f32[4,64,128]{2,1,0:T(8,128)S(1)}, u32[]{:S(2)}, u32[]{:S(2)}) async-start(f32[4,64,128]{2,1,0:T(8,128)} %get-tuple-element.11), calls=%async_computation.3 | async-start | bytes 262144 | tf_op jit(solution)/shard_map/all_to_all | solution.py:321
  66.3 4.0 %shard_map.45 = (f32[32,128]{1,0:T(8,128)S(1)}, f32[32,128]{1,0:T(8,128)S(1)}) custom-call(f32[16,128]{1,0:T(8,128)S(1)} %get-tuple-element.12.gram_ref, f32[48,128]{1,0:T(8,128)S(1)} %get-tuple-element.13.stack_ref), custom_call_target="tpu_custom_call" | custom-call | flops 500000000 | bytes 10000000 | tf_op jit(solution)/shard_map/pallas_call | solution.py:322
  70.3 4.8 %all-to-all-done.3.sums_ref = f32[4,64,128]{2,1,0:T(8,128)S(1)} async-done(((f32[4,64,128]{2,1,0:T(8,128)}), f32[4,64,128]{2,1,0:T(8,128)S(1)}, u32[]{:S(2)}, u32[]{:S(2)}) %all-to-all-start.3) | async-done | bytes 131104 | tf_op jit(solution)/shard_map/all_to_all | solution.py:321
  75.1 0.4 shard_map.46
  75.5 23.3 %all_to_all.28.got_ref = f32[32,40,128]{2,1,0:T(8,128)S(1)} all-to-all(f32[32,40,128]{2,1,0:T(8,128)S(1)} %shard_map.46), channel_id=1, replica_groups=mesh['h'=2,'y'=4,'c'=2,'x'=4,'z'=8] {'x','z'}, dimensions={0} | all-to-all | bytes 1310720 | tf_op jit(solution)/shard_map/all_to_all | solution.py:326
  98.8 1.8 %shard_map.47 = (bf16[128,5120]{1,0:T(8,128)(2,1)}, f32[2,16,5120]{2,1,0:T(8,128)}) custom-call(f32[32,40,128]{2,1,0:T(8,128)S(1)} %all_to_all.28.got_ref, bf16[128,5120]{1,0:T(8,128)(2,1)S(1)} %bitcast.12, f32[32,128]{1,0:T(8,128)S(1)} %get-tuple-element.15.basis_ref), custom_call_target="tpu_custom_call" | custom-call | tf_op jit(solution)/shard_map/pallas_call | solution.py:328
Async XLA Ops:
  0.6 5.0 %copy-start = (bf16[1,128,5120]{2,1,0:T(8,128)(2,1)S(1)}, bf16[1,128,5120]{2,1,0:T(8,128)(2,1)}, u32[]{:S(2)}) copy-start(bf16[1,128,5120]{2,1,0:T(8,128)(2,1)} %param.2) | copy-start | bytes 3932164
  1.7 3.9 %collective-permute-start = (f32[16,5120]{1,0:T(8,128)S(1)}, f32[16,5120]{1,0:T(8,128)S(1)}, u32[]{:S(2)}, u32[]{:S(2)}) collective-permute-start(f32[16,5120]{1,0:T(8,128)S(1)} %bitcast_convert_fusion), channel_id=1, source_target_pairs={{0,32},{32,0},{1,33},{33,1},{2,34},{34,2},{3,35},{35,3},{4,36},{36... | collective-permute-start | bytes 983048 | tf_op jit(solution)/shard_map/ppermute | solution.py:297
  63.0 12.1 %all-to-all-start.3 = ((f32[4,64,128]{2,1,0:T(8,128)}), f32[4,64,128]{2,1,0:T(8,128)S(1)}, u32[]{:S(2)}, u32[]{:S(2)}) async-start(f32[4,64,128]{2,1,0:T(8,128)} %get-tuple-element.11), calls=%async_computation.3 | async-start | bytes 262144 | tf_op jit(solution)/shard_map/all_to_all | solution.py:321

commit v3 on v2

--- a/solution.py
+++ b/solution.py
@@ -10,8 +10,12 @@
 
 RANK = 16
 LANES = 128
-NX, NZ = 4, 8
-TILES = 10
+FIRST, FIRST_SIZE = ("x", "v"), 8
+SECOND, SECOND_SIZE = ("w",), 4
+TILES = 40 // FIRST_SIZE
+REST = TILES - SECOND_SIZE
+OWNERS = FIRST_SIZE * SECOND_SIZE
+SPLIT_GATHER = True
 GROUP = 32
 HIGHEST = lax.Precision.HIGHEST
 F32 = jnp.float32
@@ -56,29 +60,22 @@
 
 
 def sketch_body(sketch_ref, starts_ref, weight_ref, send_ref):
-    crossed = lax.dot_general(
-        starts_ref[...].astype(BF16),
-        weight_ref[...],
-        (((1,), (1,)), ((), ())),
-        preferred_element_type=F32,
-    )
-    for n in range(4):
-        send_ref[n, 0:32, :] = sketch_ref[...]
-        send_ref[n, 32:48, :] = crossed
-
-
-def project_body(sketch_ref, weight_ref, send_ref, stack_ref):
-    half, core = lax.axis_index("h"), lax.axis_index("c")
-    even, low = signs()
-    mine = sketch_ref[2 * half + core]
-    side = sketch_ref[2 * half + 1 - core]
-    far = sketch_ref[2 * (1 - half) + core]
-    far_side = sketch_ref[2 * (1 - half) + 1 - core]
-    cross = low * (mine[16:32] - far[16:32])
-    own = even * (mine[0:16] - side[0:16])
-    other = even * (far[0:16] - far_side[0:16])
-    start_own = even * (mine[16:32] - side[32:48])
-    start_other = even * (far[16:32] - far_side[32:48])
+    send_ref[0:16, :] = sketch_ref[0:16]
+    send_ref[16:32, :] = dot_t(starts_ref[...].astype(BF16), weight_ref[...], None)
+
+
+def differ_body(sketch_ref, mine_ref, side_ref, send_ref):
+    even, _ = signs()
+    send_ref[0:16, :] = even * (mine_ref[0:16] - side_ref[0:16])
+    send_ref[16:32, :] = even * (sketch_ref[16:32] - side_ref[16:32])
+    send_ref[32:48, :] = sketch_ref[16:32]
+
+
+def project_body(mine_ref, far_ref, weight_ref, send_ref, stack_ref):
+    _, low = signs()
+    own, start_own = mine_ref[0:16], mine_ref[16:32]
+    other, start_other = far_ref[0:16], far_ref[16:32]
+    cross = low * (mine_ref[32:48] - far_ref[32:48])
     stack = jnp.concatenate([cross, own, other], axis=0)
     stack_ref[...] = stack
     zero = jnp.zeros((RANK, LANES), F32)
@@ -93,7 +90,7 @@
     )
     high, low_part = pieces(stack)
     both = jnp.concatenate([high, low_part], axis=0)
-    for x in range(NX):
+    for x in range(FIRST_SIZE):
         span = TILES * LANES
         product = jnp.dot(
             both, weight_ref[:, x * span : (x + 1) * span], preferred_element_type=F32
@@ -108,17 +105,20 @@
     return lax.broadcasted_iota(jnp.int32, (RANK, LANES), 1) // GROUP
 
 
+def added(values):
+    while len(values) > 1:
+        values = [a + b for a, b in zip(values[::2], values[1::2])]
+    return values[0]
+
+
 def first_sum_body(got_ref, send_ref):
     def total(start, size):
-        rows = pl.ds(start, size)
-        return (got_ref[0, rows, :] + got_ref[1, rows, :]) + (
-            got_ref[2, rows, :] + got_ref[3, rows, :]
-        )
+        return added([got_ref[x, start : start + size, :] for x in range(FIRST_SIZE)])
 
     gram = total(TILES * 48, 16)
     lanes = lane_group()
-    rests = [total((NZ + k) * 48, 48) for k in range(2)]
-    for z in range(NZ):
+    rests = [total((SECOND_SIZE + k) * 48, 48) for k in range(REST)]
+    for z in range(SECOND_SIZE):
         send_ref[z, 0:48, :] = total(z * 48, 48)
         k, g = z // 4, z % 4
         packed = jnp.zeros((RANK, LANES), F32)
@@ -132,13 +132,20 @@
         send_ref[z, 64:80, :] = gram
 
 
-def second_sum_body(got_ref, send_ref, gram_ref):
-    total = got_ref[0]
-    for z in range(1, NZ):
-        total = total + got_ref[z]
-    for n in range(4):
-        send_ref[n] = total[0:64]
+def second_sum_body(got_ref, sums_ref, side_ref, gram_ref):
+    total = added([got_ref[z] for z in range(SECOND_SIZE)])
+    sums_ref[...] = total[0:64]
+    side_ref[0:16, :] = total[16:32]
+    side_ref[16:32, :] = total[48:64]
     gram_ref[...] = total[64:80]
+
+
+def join_body(sums_ref, side_ref, gram_in_ref, send_ref, gram_ref):
+    moved = pltpu.roll(side_ref[16:32], 2 * GROUP, 1)
+    send_ref[0:48, :] = sums_ref[0:48]
+    send_ref[48:64, :] = jnp.where(lane_group() == 3, moved, sums_ref[48:64])
+    send_ref[64:80, :] = side_ref[0:16]
+    gram_ref[...] = gram_in_ref[...]
 
 
 def eye():
@@ -205,30 +212,19 @@
     basis_ref[...] = jnp.concatenate([basis0, basis1], axis=0)
 
 
-def combine_body(sums_ref, mix_ref, send_ref):
-    half, core = lax.axis_index("h"), lax.axis_index("c")
-    mine, side = 2 * half + core, 2 * half + 1 - core
-    far, far_side = 2 * (1 - half) + core, 2 * (1 - half) + 1 - core
-    rest, far_rest = sums_ref[mine, 48:64, :], sums_ref[far, 48:64, :]
-    side_rest, far_side_rest = sums_ref[side, 48:64, :], sums_ref[far_side, 48:64, :]
+def combine_body(sums_ref, side_ref, far_ref, mix_ref, send_ref):
+    rest, far_rest = sums_ref[48:64], far_ref[48:64]
 
     def turned(value, a):
         return pltpu.roll(value, LANES - GROUP * a, 1) if a else value
 
     main = jnp.concatenate(
-        [
-            sums_ref[mine, 0:48, :],
-            sums_ref[side, 16:32, :],
-            sums_ref[far, 0:48, :],
-            sums_ref[far_side, 16:32, :],
-        ],
-        axis=0,
+        [sums_ref[0:48], side_ref[0:16], far_ref[0:48], far_ref[64:80]], axis=0
     )
     tail = jnp.concatenate(
         [turned(rest, a) for a in range(3)]
-        + [turned(side_rest, 1)]
-        + [turned(far_rest, a) for a in range(3)]
-        + [turned(far_side_rest, 1)],
+        + [turned(side_ref[16:32], 1)]
+        + [turned(far_rest, a) for a in range(4)],
         axis=0,
     )
     mix = mix_ref[...]
@@ -238,37 +234,47 @@
     packed = tail[0:8]
     for a in range(1, 4):
         packed = jnp.where(lanes == a, pltpu.roll(tail[8 * a : 8 * a + 8], GROUP * a, 1), packed)
-    for n in range(NX * NZ):
+    for n in range(send_ref.shape[0]):
         send_ref[n, 0:32, :] = head
         send_ref[n, 32:40, :] = packed
+
+
+def spread_body(got_ref, send_ref):
+    for n in range(FIRST_SIZE):
+        for z in range(SECOND_SIZE):
+            send_ref[n, z * 40 : (z + 1) * 40, :] = got_ref[z]
 
 
 def update_body(
     got_ref, weight_ref, basis_ref, corrected_hbm, factors_hbm, corrected_ref, factors_ref, sems
 ):
     lanes = lane_group()[0:8]
-    span = TILES * LANES
+    chunk = 10
+    span = chunk * LANES
     transposed = basis_ref[...].T
     left = []
     for k in range(2):
         high, low = pieces(transposed[:, 16 * k : 16 * k + 16])
         left.append(jnp.concatenate([high, low, high], axis=1))
     copies = []
-    for x in range(NX):
-        tiles = [got_ref[x * NZ + z, 0:32, :] for z in range(NZ)]
-        for k in range(2):
-            groups = []
-            for a in range(4):
-                row = None
-                for g in range(4):
-                    piece = got_ref[x * NZ + 4 * k + g, 32:40, :]
-                    shift = (GROUP * (g - a)) % LANES
-                    if shift:
-                        piece = pltpu.roll(piece, shift, 1)
-                    row = piece if row is None else jnp.where(lanes == g, piece, row)
-                groups.append(row)
-            tiles.append(jnp.concatenate(groups, axis=0))
-        for t in range(0, TILES, 2):
+    for x in range(4):
+        tiles = []
+        for first in range(x * FIRST_SIZE // 4, (x + 1) * FIRST_SIZE // 4):
+            base = first * SECOND_SIZE
+            tiles += [got_ref[base + z, 0:32, :] for z in range(SECOND_SIZE)]
+            for k in range(REST):
+                groups = []
+                for a in range(4):
+                    row = None
+                    for g in range(4):
+                        piece = got_ref[base + 4 * k + g, 32:40, :]
+                        shift = (GROUP * (g - a)) % LANES
+                        if shift:
+                            piece = pltpu.roll(piece, shift, 1)
+                        row = piece if row is None else jnp.where(lanes == g, piece, row)
+                    groups.append(row)
+                tiles.append(jnp.concatenate(groups, axis=0))
+        for t in range(0, chunk, 2):
             part = pl.ds(x * span + t * LANES, 2 * LANES)
             pair = jnp.concatenate(tiles[t : t + 2], axis=1)
             current = weight_ref[:, part].astype(F32)
@@ -308,22 +314,33 @@
         (((1,), (1,)), ((), ())),
         preferred_element_type=F32,
     )
-    sketch = call(sketch_body, shape(4, 48, rows), 3)(sketch, swapped, weight)
-    sketch = lax.all_to_all(sketch, ("h", "c"), 0, 0)
+    mine = call(sketch_body, shape(32, rows), 3)(sketch, swapped, weight)
+    mine = call(differ_body, shape(48, rows), 3)(sketch, mine, flip(mine, "c"))
+    far = flip(mine, "h")
     depth = TILES * 48 + 16
     send, stack = call(
-        project_body, (shape(NX, depth, LANES), shape(48, LANES)), 2, 130_000_000, 4_000_000
-    )(sketch, weight)
-    got = lax.all_to_all(send, "x", 0, 0)
-    send = call(first_sum_body, shape(NZ, 80, LANES), 1)(got)
-    got = lax.all_to_all(send, "z", 0, 0)
-    send, gram = call(second_sum_body, (shape(4, 64, LANES), shape(16, LANES)), 1)(got)
-    sums = lax.all_to_all(send, ("h", "c"), 0, 0)
+        project_body, (shape(FIRST_SIZE, depth, LANES), shape(48, LANES)), 3, 130_000_000, 4_000_000
+    )(mine, far, weight)
+    got = lax.all_to_all(send, FIRST, 0, 0)
+    send = call(first_sum_body, shape(SECOND_SIZE, 80, LANES), 1)(got)
+    got = lax.all_to_all(send, SECOND, 0, 0)
+    sums, side, gram = call(
+        second_sum_body, (shape(64, LANES), shape(32, LANES), shape(16, LANES)), 1
+    )(got)
+    side = flip(side, "c")
+    send, gram = call(join_body, (shape(80, LANES), shape(16, LANES)), 3)(sums, side, gram)
+    far = flip(send, "h")
     mix, basis = call(
         factor_body, (shape(32, LANES), shape(32, LANES)), 2, 500_000_000, 10_000_000
     )(gram, stack)
-    send = call(combine_body, shape(NX * NZ, 40, LANES), 2)(sums, mix)
-    got = lax.all_to_all(send, ("x", "z"), 0, 0)
+    copies = SECOND_SIZE if SPLIT_GATHER else OWNERS
+    send = call(combine_body, shape(copies, 40, LANES), 4)(sums, side, far, mix)
+    if SPLIT_GATHER:
+        got = lax.all_to_all(send, SECOND, 0, 0)
+        send = call(spread_body, shape(FIRST_SIZE, SECOND_SIZE * 40, LANES), 1)(got)
+        got = lax.all_to_all(send, FIRST, 0, 0).reshape(OWNERS, 40, LANES)
+    else:
+        got = lax.all_to_all(send, FIRST + SECOND, 0, 0)
     hbm = pl.BlockSpec(memory_space=pltpu.HBM)
     corrected, factors = pl.pallas_call(
         update_body,
@@ -333,7 +350,7 @@
         scratch_shapes=[
             pltpu.VMEM((rows, cols), BF16),
             pltpu.VMEM((2, RANK, cols), F32),
-            pltpu.SemaphoreType.DMA((2 * NX,)),
+            pltpu.SemaphoreType.DMA((8,)),
         ],
         compiler_params=pltpu.CompilerParams(vmem_limit_bytes=40 * 2**20),
     )(got, weight, basis)
@@ -341,8 +358,8 @@
 
 
 def solution(mesh):
-    inner = Mesh(mesh.devices.reshape(2, 4, 2, NX, NZ), ("h", "y", "c", "x", "z"))
-    placed = (P(("h", "y", "c"), ("x", "z"), None), P(("h", "y", "c"), None, None, None))
+    inner = Mesh(mesh.devices.reshape(2, 4, 2, 4, 4, 2), ("h", "y", "c", "x", "w", "v"))
+    placed = (P(("h", "y", "c"), ("x", "w", "v"), None), P(("h", "y", "c"), None, None, None))
     return jax.shard_map(
         shards, mesh=inner, in_specs=placed, out_specs=placed, check_vma=False
     )

time: 101 us -> 99.1 us (0.981)
  blocking collectives: 78.8 us -> 62.9 us
  starting transfers between devices: 5.25 us -> 19.9 us
    ppermute x1 -> x5, starting transfers between devices: 1.92 us -> 19.9 us  [flip(): return lax.ppermute(value, axis, [(0, 1), (1, 0)])]
    all_to_all x4, blocking collectives: 78.8 us -> 62.9 us  [the longest x2 28.9 us: shards(): got = lax.all_to_all(send, SECOND, 0, 0)]
    all_to_all x1 -> x0, waiting for transfers between devices: 4.83 us -> none  [shards(): sums = lax.all_to_all(send, ('h', 'c'), 0, 0)]
    ppermute x1 -> x5, waiting for transfers between devices: 0.02 us -> 4.78 us  [flip(): return lax.ppermute(value, axis, [(0, 1), (1, 0)])]
    all_to_all x1 -> x0, starting transfers between devices: 3.33 us -> none  [shards(): sums = lax.all_to_all(send, ('h', 'c'), 0, 0)]
    pallas_call x5 -> x8, Pallas kernels: 2.19 us -> 1.63 us  [the longest x1 0.62 us: shards(): call(project_body, (shape(FIRST_SIZE, depth, LANES), shape(48, LANES)), 3...]
  transfers between devices with their start and end apart: 2 -> 5, of which waited for: 1 -> 3; matrix products, arithmetic and copies ran while one was open for 2% -> 2% of each run, Pallas kernels for 4% -> 4%
where the time goes in v3:
time: 99.1 us; the launch traced here: 98.7 us
  blocking collectives  62.9 us (63%)
  starting transfers between devices  19.9 us (20%)
  Pallas kernels  7.42 us (7%)
  waiting for transfers between devices  4.78 us (5%)
  matrix products  1.95 us (2%)
  other arithmetic  1.04 us (1%)
    all_to_all x2, blocking collectives, shards(): got = lax.all_to_all(send, SECOND, 0, 0)  28.9 us
    all_to_all x1, blocking collectives, shards(): got = lax.all_to_all(send, FIRST, 0, 0)  21 us
    ppermute x5, starting transfers between devices, flip(): return lax.ppermute(value, axis, [(0, 1), (1, 0)])  19.9 us
    all_to_all x1, blocking collectives, shards(): got = lax.all_to_all(send, FIRST, 0, 0).reshape(OWNERS, 40, LANES)  13 us
    ppermute x5, waiting for transfers between devices, flip(): return lax.ppermute(value, axis, [(0, 1), (1, 0)])  4.78 us
    pallas_call x1, Pallas kernels, shards(): call(factor_body, (shape(32, LANES), shape(32, LANES)), 2, 500000000, 100...  3.97 us
  transfers between devices with their start and end apart: 5, of which 3 were waited for; matrix products, arithmetic and copies ran while one was open for 2% of the time, Pallas kernels for 4%

profile of v3, /device:TPU:8, one launch (start us, length us, event | category | flops | bytes accessed | tf_op | source)
XLA Modules:
  0.0 98.7 jit_solution(5423206374206438622)
XLA Ops:
  0.6 0.0 copy-start
  0.6 1.0 %bitcast_convert_fusion = f32[16,5120]{1,0:T(8,128)S(1)} fusion(bf16[1,2,16,5120]{3,2,1,0:T(8,128)(2,1)} %param.3), kind=kLoop, calls=%fused_computation | loop fusion | flops 81920 | bytes 491520 | tf_op jit(solution)/shard_map/convert_element_type | solution.py:310
  1.7 1.9 %collective-permute-start = (f32[16,5120]{1,0:T(8,128)S(1)}, f32[16,5120]{1,0:T(8,128)S(1)}, u32[]{:S(2)}, u32[]{:S(2)}) collective-permute-start(f32[16,5120]{1,0:T(8,128)S(1)} %bitcast_convert_fusion), channel_id=1, source_target_pairs={{0,32},{32,0},{1,33},{33,1},{2,34},{34,2},{3,35},{35,3},{4,36},{36... | collective-permute-start | bytes 983048 | tf_op jit(solution)/shard_map/ppermute | solution.py:303
  3.6 2.0 %fusion.sketch_ref = f32[32,128]{1,0:T(8,128)S(1)} fusion(bf16[32,5120]{1,0:T(8,128)(2,1)} %bitcast.15, bf16[1,128,5120]{2,1,0:T(8,128)(2,1)} %param.2), kind=kOutput, calls=%fused_computation.1 | convolution fusion | flops 41943040 | bytes 1654784 | tf_op jit(solution)/shard_map/dot_general | solution.py:311
  5.6 0.0 collective-permute-done.starts_ref
  5.6 0.0 copy-done
  5.6 0.4 shard_map.41.mine_ref
  6.0 2.4 %collective-permute-start.1 = (f32[32,128]{1,0:T(8,128)S(1)}, f32[32,128]{1,0:T(8,128)S(1)}, u32[]{:S(2)}, u32[]{:S(2)}) collective-permute-start(f32[32,128]{1,0:T(8,128)S(1)} %shard_map.41.mine_ref), channel_id=1, source_target_pairs={{0,32},{32,0},{1,33},{33,1},{2,34},{34,2},{3,35},{35,3},{4,36},{36... | collective-permute-start | bytes 49160 | tf_op jit(solution)/shard_map/ppermute | solution.py:303
  8.5 0.8 collective-permute-done.1.side_ref
  9.3 6.8 %collective-permute-start.2 = (f32[48,128]{1,0:T(8,128)S(1)}, f32[48,128]{1,0:T(8,128)S(1)}, u32[]{:S(2)}, u32[]{:S(2)}) collective-permute-start(f32[48,128]{1,0:T(8,128)S(1)} %shard_map.42.mine_ref), channel_id=1, source_target_pairs={{0,256},{256,0},{1,257},{257,1},{2,258},{258,2},{3,259},{259,3},{4... | collective-permute-start | bytes 73736 | tf_op jit(solution)/shard_map/ppermute | solution.py:303
  16.1 2.8 %collective-permute-done.2.far_ref = f32[48,128]{1,0:T(8,128)S(1)} collective-permute-done((f32[48,128]{1,0:T(8,128)S(1)}, f32[48,128]{1,0:T(8,128)S(1)}, u32[]{:S(2)}, u32[]{:S(2)}) %collective-permute-start.2) | collective-permute-done | bytes 24608 | tf_op jit(solution)/shard_map/ppermute | solution.py:303
  18.9 0.6 shard_map.43
  19.5 21.0 %all_to_all.20.got_ref = f32[8,256,128]{2,1,0:T(8,128)S(1)} all-to-all(f32[8,256,128]{2,1,0:T(8,128)S(1)} %get-tuple-element.13), channel_id=1, replica_groups=mesh['h'=2,'y'=4,'c'=2,'x'=4,'w'=4,'v'=2] {'x','v'}, dimensions={0} | all-to-all | bytes 2097152 | tf_op jit(solution)/shard_map/all_to_all | solution.py:324
  40.5 0.1 shard_map.44
  40.6 18.2 %all_to_all.21.got_ref = f32[4,80,128]{2,1,0:T(8,128)S(1)} all-to-all(f32[4,80,128]{2,1,0:T(8,128)S(1)} %shard_map.44), channel_id=1, replica_groups=mesh['h'=2,'y'=4,'c'=2,'x'=4,'w'=4,'v'=2] {'w'}, dimensions={0} | all-to-all | bytes 327680 | tf_op jit(solution)/shard_map/all_to_all | solution.py:326
  58.8 1.9 %collective-permute-start.3 = (f32[32,128]{1,0:T(8,128)S(1)}, f32[32,128]{1,0:T(8,128)S(1)}, u32[]{:S(2)}, u32[]{:S(2)}) collective-permute-start(f32[32,128]{1,0:T(8,128)S(1)} %get-tuple-element.15), channel_id=1, source_target_pairs={{0,32},{32,0},{1,33},{33,1},{2,34},{34,2},{3,35},{35,3},{4,36},{36... | collective-permute-start | bytes 49160 | tf_op jit(solution)/shard_map/ppermute | solution.py:303
  60.8 1.1 %collective-permute-done.3.side_ref = f32[32,128]{1,0:T(8,128)S(1)} collective-permute-done((f32[32,128]{1,0:T(8,128)S(1)}, f32[32,128]{1,0:T(8,128)S(1)}, u32[]{:S(2)}, u32[]{:S(2)}) %collective-permute-start.3) | collective-permute-done | bytes 16416 | tf_op jit(solution)/shard_map/ppermute | solution.py:303
  61.9 0.1 shard_map.46
  62.0 6.8 %collective-permute-start.4 = (f32[80,128]{1,0:T(8,128)S(1)}, f32[80,128]{1,0:T(8,128)S(1)}, u32[]{:S(2)}, u32[]{:S(2)}) collective-permute-start(f32[80,128]{1,0:T(8,128)S(1)} %get-tuple-element.17), channel_id=1, source_target_pairs={{0,256},{256,0},{1,257},{257,1},{2,258},{258,2},{3,259},{259,3},{4... | collective-permute-start | bytes 122888 | tf_op jit(solution)/shard_map/ppermute | solution.py:303
  68.8 4.0 %shard_map.47 = (f32[32,128]{1,0:T(8,128)S(1)}, f32[32,128]{1,0:T(8,128)S(1)}) custom-call(f32[16,128]{1,0:T(8,128)S(1)} %get-tuple-element.18.gram_ref, f32[48,128]{1,0:T(8,128)S(1)} %get-tuple-element.19.stack_ref), custom_call_target="tpu_custom_call" | custom-call | flops 500000000 | bytes 10000000 | tf_op jit(solution)/shard_map/pallas_call | solution.py:333
  72.8 0.0 collective-permute-done.4.far_ref
  72.8 0.4 shard_map.48
  73.1 10.7 %all_to_all.22.got_ref = f32[4,40,128]{2,1,0:T(8,128)S(1)} all-to-all(f32[4,40,128]{2,1,0:T(8,128)S(1)} %shard_map.48), channel_id=1, replica_groups=mesh['h'=2,'y'=4,'c'=2,'x'=4,'w'=4,'v'=2] {'w'}, dimensions={0} | all-to-all | bytes 163840 | tf_op jit(solution)/shard_map/all_to_all | solution.py:339
  83.9 13.0 %all_to_all.23 = f32[8,160,128]{2,1,0:T(8,128)S(1)} all-to-all(f32[8,160,128]{2,1,0:T(8,128)S(1)} %shard_map.49), channel_id=1, replica_groups=mesh['h'=2,'y'=4,'c'=2,'x'=4,'w'=4,'v'=2] {'x','v'}, dimensions={0} | all-to-all | bytes 1310720 | tf_op jit(solution)/shard_map/all_to_all | solution.py:341
  96.9 1.8 %shard_map.50 = (bf16[128,5120]{1,0:T(8,128)(2,1)}, f32[2,16,5120]{2,1,0:T(8,128)}) custom-call(f32[32,40,128]{2,1,0:T(8,128)S(1)} %bitcast.14, bf16[128,5120]{1,0:T(8,128)(2,1)S(1)} %bitcast.13, f32[32,128]{1,0:T(8,128)S(1)} %get-tuple-element.21.basis_ref), custom_call_target="tpu_custom_call" | custom-call | tf_op jit(solution)/shard_map/pallas_call | solution.py:345
  (3 shorter events, 0.1 us)
Async XLA Ops:
  0.6 5.0 %copy-start = (bf16[1,128,5120]{2,1,0:T(8,128)(2,1)S(1)}, bf16[1,128,5120]{2,1,0:T(8,128)(2,1)}, u32[]{:S(2)}) copy-start(bf16[1,128,5120]{2,1,0:T(8,128)(2,1)} %param.2) | copy-start | bytes 3932164
  1.7 3.9 %collective-permute-start = (f32[16,5120]{1,0:T(8,128)S(1)}, f32[16,5120]{1,0:T(8,128)S(1)}, u32[]{:S(2)}, u32[]{:S(2)}) collective-permute-start(f32[16,5120]{1,0:T(8,128)S(1)} %bitcast_convert_fusion), channel_id=1, source_target_pairs={{0,32},{32,0},{1,33},{33,1},{2,34},{34,2},{3,35},{35,3},{4,36},{36... | collective-permute-start | bytes 983048 | tf_op jit(solution)/shard_map/ppermute | solution.py:303
  6.0 3.3 %collective-permute-start.1 = (f32[32,128]{1,0:T(8,128)S(1)}, f32[32,128]{1,0:T(8,128)S(1)}, u32[]{:S(2)}, u32[]{:S(2)}) collective-permute-start(f32[32,128]{1,0:T(8,128)S(1)} %shard_map.41.mine_ref), channel_id=1, source_target_pairs={{0,32},{32,0},{1,33},{33,1},{2,34},{34,2},{3,35},{35,3},{4,36},{36... | collective-permute-start | bytes 49160 | tf_op jit(solution)/shard_map/ppermute | solution.py:303
  9.3 9.6 %collective-permute-start.2 = (f32[48,128]{1,0:T(8,128)S(1)}, f32[48,128]{1,0:T(8,128)S(1)}, u32[]{:S(2)}, u32[]{:S(2)}) collective-permute-start(f32[48,128]{1,0:T(8,128)S(1)} %shard_map.42.mine_ref), channel_id=1, source_target_pairs={{0,256},{256,0},{1,257},{257,1},{2,258},{258,2},{3,259},{259,3},{4... | collective-permute-start | bytes 73736 | tf_op jit(solution)/shard_map/ppermute | solution.py:303
  58.8 3.1 %collective-permute-start.3 = (f32[32,128]{1,0:T(8,128)S(1)}, f32[32,128]{1,0:T(8,128)S(1)}, u32[]{:S(2)}, u32[]{:S(2)}) collective-permute-start(f32[32,128]{1,0:T(8,128)S(1)} %get-tuple-element.15), channel_id=1, source_target_pairs={{0,32},{32,0},{1,33},{33,1},{2,34},{34,2},{3,35},{35,3},{4,36},{36... | collective-permute-start | bytes 49160 | tf_op jit(solution)/shard_map/ppermute | solution.py:303
  62.0 10.8 %collective-permute-start.4 = (f32[80,128]{1,0:T(8,128)S(1)}, f32[80,128]{1,0:T(8,128)S(1)}, u32[]{:S(2)}, u32[]{:S(2)}) collective-permute-start(f32[80,128]{1,0:T(8,128)S(1)} %get-tuple-element.17), channel_id=1, source_target_pairs={{0,256},{256,0},{1,257},{257,1},{2,258},{258,2},{3,259},{259,3},{4... | collective-permute-start | bytes 122888 | tf_op jit(solution)/shard_map/ppermute | solution.py:303

commit v4 on v3

--- a/solution.py
+++ b/solution.py
@@ -15,7 +15,6 @@
 TILES = 40 // FIRST_SIZE
 REST = TILES - SECOND_SIZE
 OWNERS = FIRST_SIZE * SECOND_SIZE
-SPLIT_GATHER = True
 GROUP = 32
 HIGHEST = lax.Precision.HIGHEST
 F32 = jnp.float32
@@ -237,12 +236,6 @@
     for n in range(send_ref.shape[0]):
         send_ref[n, 0:32, :] = head
         send_ref[n, 32:40, :] = packed
-
-
-def spread_body(got_ref, send_ref):
-    for n in range(FIRST_SIZE):
-        for z in range(SECOND_SIZE):
-            send_ref[n, z * 40 : (z + 1) * 40, :] = got_ref[z]
 
 
 def update_body(
@@ -333,14 +326,8 @@
     mix, basis = call(
         factor_body, (shape(32, LANES), shape(32, LANES)), 2, 500_000_000, 10_000_000
     )(gram, stack)
-    copies = SECOND_SIZE if SPLIT_GATHER else OWNERS
-    send = call(combine_body, shape(copies, 40, LANES), 4)(sums, side, far, mix)
-    if SPLIT_GATHER:
-        got = lax.all_to_all(send, SECOND, 0, 0)
-        send = call(spread_body, shape(FIRST_SIZE, SECOND_SIZE * 40, LANES), 1)(got)
-        got = lax.all_to_all(send, FIRST, 0, 0).reshape(OWNERS, 40, LANES)
-    else:
-        got = lax.all_to_all(send, FIRST + SECOND, 0, 0)
+    send = call(combine_body, shape(OWNERS, 40, LANES), 4)(sums, side, far, mix)
+    got = lax.all_to_all(send, FIRST + SECOND, 0, 0)
     hbm = pl.BlockSpec(memory_space=pltpu.HBM)
     corrected, factors = pl.pallas_call(
         update_body,

time: 99.1 us -> 98.4 us (level)
  the two profiles are of different devices: /device:TPU:8 before, /device:TPU:2 now
where the time goes in v4:
time: 98.4 us; the launch traced here: 98 us
  blocking collectives  61.3 us (62%)
  starting transfers between devices  21.7 us (22%)
  Pallas kernels  7.4 us (8%)
  waiting for transfers between devices  3.88 us (4%)
  matrix products  1.95 us (2%)
  other arithmetic  1.04 us (1%)
    all_to_all x1, blocking collectives, shards(): got = lax.all_to_all(send, FIRST + SECOND, 0, 0)  23.2 us
    all_to_all x1, blocking collectives, shards(): got = lax.all_to_all(send, FIRST, 0, 0)  21.9 us
    ppermute x5, starting transfers between devices, flip(): return lax.ppermute(value, axis, [(0, 1), (1, 0)])  21.7 us
    all_to_all x1, blocking collectives, shards(): got = lax.all_to_all(send, SECOND, 0, 0)  16.2 us
    pallas_call x1, Pallas kernels, shards(): call(factor_body, (shape(32, LANES), shape(32, LANES)), 2, 500000000, 100...  3.97 us
    ppermute x5, waiting for transfers between devices, flip(): return lax.ppermute(value, axis, [(0, 1), (1, 0)])  3.88 us
  transfers between devices with their start and end apart: 5, of which 3 were waited for; matrix products, arithmetic and copies ran while one was open for 2% of the time, Pallas kernels for 4%

profile of v4, /device:TPU:2, one launch (start us, length us, event | category | flops | bytes accessed | tf_op | source)
XLA Modules:
  0.0 98.0 jit_solution(17610099944717264040)
XLA Ops:
  0.6 0.0 copy-start
  0.6 1.0 %bitcast_convert_fusion = f32[16,5120]{1,0:T(8,128)S(1)} fusion(bf16[1,2,16,5120]{3,2,1,0:T(8,128)(2,1)} %param.3), kind=kLoop, calls=%fused_computation | loop fusion | flops 81920 | bytes 491520 | tf_op jit(solution)/shard_map/convert_element_type | solution.py:303
  1.7 1.9 %collective-permute-start = (f32[16,5120]{1,0:T(8,128)S(1)}, f32[16,5120]{1,0:T(8,128)S(1)}, u32[]{:S(2)}, u32[]{:S(2)}) collective-permute-start(f32[16,5120]{1,0:T(8,128)S(1)} %bitcast_convert_fusion), channel_id=1, source_target_pairs={{0,32},{32,0},{1,33},{33,1},{2,34},{34,2},{3,35},{35,3},{4,36},{36... | collective-permute-start | bytes 983048 | tf_op jit(solution)/shard_map/ppermute | solution.py:296
  3.6 1.9 %fusion.sketch_ref = f32[32,128]{1,0:T(8,128)S(1)} fusion(bf16[32,5120]{1,0:T(8,128)(2,1)} %bitcast.13, bf16[1,128,5120]{2,1,0:T(8,128)(2,1)} %param.2), kind=kOutput, calls=%fused_computation.1 | convolution fusion | flops 41943040 | bytes 1654784 | tf_op jit(solution)/shard_map/dot_general | solution.py:304
  5.6 0.0 collective-permute-done.starts_ref
  5.6 0.0 copy-done
  5.6 0.4 shard_map.41.mine_ref
  6.0 2.4 %collective-permute-start.1 = (f32[32,128]{1,0:T(8,128)S(1)}, f32[32,128]{1,0:T(8,128)S(1)}, u32[]{:S(2)}, u32[]{:S(2)}) collective-permute-start(f32[32,128]{1,0:T(8,128)S(1)} %shard_map.41.mine_ref), channel_id=1, source_target_pairs={{0,32},{32,0},{1,33},{33,1},{2,34},{34,2},{3,35},{35,3},{4,36},{36... | collective-permute-start | bytes 49160 | tf_op jit(solution)/shard_map/ppermute | solution.py:296
  8.5 0.8 collective-permute-done.1.side_ref
  9.3 7.7 %collective-permute-start.2 = (f32[48,128]{1,0:T(8,128)S(1)}, f32[48,128]{1,0:T(8,128)S(1)}, u32[]{:S(2)}, u32[]{:S(2)}) collective-permute-start(f32[48,128]{1,0:T(8,128)S(1)} %shard_map.42.mine_ref), channel_id=1, source_target_pairs={{0,256},{256,0},{1,257},{257,1},{2,258},{258,2},{3,259},{259,3},{4... | collective-permute-start | bytes 73736 | tf_op jit(solution)/shard_map/ppermute | solution.py:296
  17.0 1.9 %collective-permute-done.2.far_ref = f32[48,128]{1,0:T(8,128)S(1)} collective-permute-done((f32[48,128]{1,0:T(8,128)S(1)}, f32[48,128]{1,0:T(8,128)S(1)}, u32[]{:S(2)}, u32[]{:S(2)}) %collective-permute-start.2) | collective-permute-done | bytes 24608 | tf_op jit(solution)/shard_map/ppermute | solution.py:296
  18.9 0.6 shard_map.43
  19.5 21.9 %all_to_all.15.got_ref = f32[8,256,128]{2,1,0:T(8,128)S(1)} all-to-all(f32[8,256,128]{2,1,0:T(8,128)S(1)} %get-tuple-element.13), channel_id=1, replica_groups=mesh['h'=2,'y'=4,'c'=2,'x'=4,'w'=4,'v'=2] {'x','v'}, dimensions={0} | all-to-all | bytes 2097152 | tf_op jit(solution)/shard_map/all_to_all | solution.py:317
  41.4 0.1 shard_map.44
  41.5 16.2 %all_to_all.16.got_ref = f32[4,80,128]{2,1,0:T(8,128)S(1)} all-to-all(f32[4,80,128]{2,1,0:T(8,128)S(1)} %shard_map.44), channel_id=1, replica_groups=mesh['h'=2,'y'=4,'c'=2,'x'=4,'w'=4,'v'=2] {'w'}, dimensions={0} | all-to-all | bytes 327680 | tf_op jit(solution)/shard_map/all_to_all | solution.py:319
  57.8 1.9 %collective-permute-start.3 = (f32[32,128]{1,0:T(8,128)S(1)}, f32[32,128]{1,0:T(8,128)S(1)}, u32[]{:S(2)}, u32[]{:S(2)}) collective-permute-start(f32[32,128]{1,0:T(8,128)S(1)} %get-tuple-element.15), channel_id=1, source_target_pairs={{0,32},{32,0},{1,33},{33,1},{2,34},{34,2},{3,35},{35,3},{4,36},{36... | collective-permute-start | bytes 49160 | tf_op jit(solution)/shard_map/ppermute | solution.py:296
  59.7 1.1 %collective-permute-done.3.side_ref = f32[32,128]{1,0:T(8,128)S(1)} collective-permute-done((f32[32,128]{1,0:T(8,128)S(1)}, f32[32,128]{1,0:T(8,128)S(1)}, u32[]{:S(2)}, u32[]{:S(2)}) %collective-permute-start.3) | collective-permute-done | bytes 16416 | tf_op jit(solution)/shard_map/ppermute | solution.py:296
  60.9 0.1 shard_map.46
  60.9 7.7 %collective-permute-start.4 = (f32[80,128]{1,0:T(8,128)S(1)}, f32[80,128]{1,0:T(8,128)S(1)}, u32[]{:S(2)}, u32[]{:S(2)}) collective-permute-start(f32[80,128]{1,0:T(8,128)S(1)} %get-tuple-element.17), channel_id=1, source_target_pairs={{0,256},{256,0},{1,257},{257,1},{2,258},{258,2},{3,259},{259,3},{4... | collective-permute-start | bytes 122888 | tf_op jit(solution)/shard_map/ppermute | solution.py:296
  68.6 4.0 %shard_map.47 = (f32[32,128]{1,0:T(8,128)S(1)}, f32[32,128]{1,0:T(8,128)S(1)}) custom-call(f32[16,128]{1,0:T(8,128)S(1)} %get-tuple-element.18.gram_ref, f32[48,128]{1,0:T(8,128)S(1)} %get-tuple-element.19.stack_ref), custom_call_target="tpu_custom_call" | custom-call | flops 500000000 | bytes 10000000 | tf_op jit(solution)/shard_map/pallas_call | solution.py:326
  72.6 0.0 collective-permute-done.4.far_ref
  72.6 0.4 shard_map.48
  73.0 23.2 %all_to_all.17.got_ref = f32[32,40,128]{2,1,0:T(8,128)S(1)} all-to-all(f32[32,40,128]{2,1,0:T(8,128)S(1)} %shard_map.48), channel_id=1, replica_groups=mesh['h'=2,'y'=4,'c'=2,'x'=4,'w'=4,'v'=2] {'x','v','w'}, dimensions={0} | all-to-all | bytes 1310720 | tf_op jit(solution)/shard_map/all_to_all | solution.py:330
  96.2 1.8 %shard_map.49 = (bf16[128,5120]{1,0:T(8,128)(2,1)}, f32[2,16,5120]{2,1,0:T(8,128)}) custom-call(f32[32,40,128]{2,1,0:T(8,128)S(1)} %all_to_all.17.got_ref, bf16[128,5120]{1,0:T(8,128)(2,1)S(1)} %bitcast.12, f32[32,128]{1,0:T(8,128)S(1)} %get-tuple-element.21.basis_ref), custom_call_target="tpu_custom_call" | custom-call | tf_op jit(solution)/shard_map/pallas_call | solution.py:332
  (2 shorter events, 0.0 us)
Async XLA Ops:
  0.6 5.0 %copy-start = (bf16[1,128,5120]{2,1,0:T(8,128)(2,1)S(1)}, bf16[1,128,5120]{2,1,0:T(8,128)(2,1)}, u32[]{:S(2)}) copy-start(bf16[1,128,5120]{2,1,0:T(8,128)(2,1)} %param.2) | copy-start | bytes 3932164
  1.7 3.9 %collective-permute-start = (f32[16,5120]{1,0:T(8,128)S(1)}, f32[16,5120]{1,0:T(8,128)S(1)}, u32[]{:S(2)}, u32[]{:S(2)}) collective-permute-start(f32[16,5120]{1,0:T(8,128)S(1)} %bitcast_convert_fusion), channel_id=1, source_target_pairs={{0,32},{32,0},{1,33},{33,1},{2,34},{34,2},{3,35},{35,3},{4,36},{36... | collective-permute-start | bytes 983048 | tf_op jit(solution)/shard_map/ppermute | solution.py:296
  6.0 3.2 %collective-permute-start.1 = (f32[32,128]{1,0:T(8,128)S(1)}, f32[32,128]{1,0:T(8,128)S(1)}, u32[]{:S(2)}, u32[]{:S(2)}) collective-permute-start(f32[32,128]{1,0:T(8,128)S(1)} %shard_map.41.mine_ref), channel_id=1, source_target_pairs={{0,32},{32,0},{1,33},{33,1},{2,34},{34,2},{3,35},{35,3},{4,36},{36... | collective-permute-start | bytes 49160 | tf_op jit(solution)/shard_map/ppermute | solution.py:296
  9.3 9.6 %collective-permute-start.2 = (f32[48,128]{1,0:T(8,128)S(1)}, f32[48,128]{1,0:T(8,128)S(1)}, u32[]{:S(2)}, u32[]{:S(2)}) collective-permute-start(f32[48,128]{1,0:T(8,128)S(1)} %shard_map.42.mine_ref), channel_id=1, source_target_pairs={{0,256},{256,0},{1,257},{257,1},{2,258},{258,2},{3,259},{259,3},{4... | collective-permute-start | bytes 73736 | tf_op jit(solution)/shard_map/ppermute | solution.py:296
  57.8 3.1 %collective-permute-start.3 = (f32[32,128]{1,0:T(8,128)S(1)}, f32[32,128]{1,0:T(8,128)S(1)}, u32[]{:S(2)}, u32[]{:S(2)}) collective-permute-start(f32[32,128]{1,0:T(8,128)S(1)} %get-tuple-element.15), channel_id=1, source_target_pairs={{0,32},{32,0},{1,33},{33,1},{2,34},{34,2},{3,35},{35,3},{4,36},{36... | collective-permute-start | bytes 49160 | tf_op jit(solution)/shard_map/ppermute | solution.py:296
  60.9 11.7 %collective-permute-start.4 = (f32[80,128]{1,0:T(8,128)S(1)}, f32[80,128]{1,0:T(8,128)S(1)}, u32[]{:S(2)}, u32[]{:S(2)}) collective-permute-start(f32[80,128]{1,0:T(8,128)S(1)} %get-tuple-element.17), channel_id=1, source_target_pairs={{0,256},{256,0},{1,257},{257,1},{2,258},{258,2},{3,259},{259,3},{4... | collective-permute-start | bytes 122888 | tf_op jit(solution)/shard_map/ppermute | solution.py:296

commit v5 on v4

--- a/solution.py
+++ b/solution.py
@@ -10,7 +10,7 @@
 
 RANK = 16
 LANES = 128
-FIRST, FIRST_SIZE = ("x", "v"), 8
+FIRST, FIRST_SIZE = ("v", "x"), 8
 SECOND, SECOND_SIZE = ("w",), 4
 TILES = 40 // FIRST_SIZE
 REST = TILES - SECOND_SIZE
@@ -280,14 +280,18 @@
                 rounded = (current - change).astype(BF16)
                 current = rounded.astype(F32)
             corrected_ref[:, part] = rounded
-        part = pl.ds(x * span, span)
-        for i, (source, target) in enumerate(
-            ((corrected_ref, corrected_hbm), (factors_ref, factors_hbm))
-        ):
-            index = (slice(None),) * (1 + i) + (part,)
-            copy = pltpu.make_async_copy(source.at[index], target.at[index], sems.at[2 * x + i])
-            copy.start()
-            copies.append(copy)
+            if t % 4 == 0 and t < 8:
+                continue
+            first, size = (x * span + (t - 2) * LANES, 4) if t < 8 else (x * span + t * LANES, 2)
+            part = pl.ds(first, size * LANES)
+            for i, (source, target) in enumerate(
+                ((corrected_ref, corrected_hbm), (factors_ref, factors_hbm))
+            ):
+                index = (slice(None),) * (1 + i) + (part,)
+                sem = sems.at[len(copies)]
+                copy = pltpu.make_async_copy(source.at[index], target.at[index], sem)
+                copy.start()
+                copies.append(copy)
     for copy in copies:
         copy.wait()
 
@@ -337,7 +341,7 @@
         scratch_shapes=[
             pltpu.VMEM((rows, cols), BF16),
             pltpu.VMEM((2, RANK, cols), F32),
-            pltpu.SemaphoreType.DMA((8,)),
+            pltpu.SemaphoreType.DMA((24,)),
         ],
         compiler_params=pltpu.CompilerParams(vmem_limit_bytes=40 * 2**20),
     )(got, weight, basis)

time: 98.4 us -> 98.5 us (level)
  the two profiles are of different devices: /device:TPU:2 before, /device:TPU:4 now
where the time goes in v5:
time: 98.5 us; the launch traced here: 98.1 us
  blocking collectives  61.4 us (62%)
  starting transfers between devices  21.7 us (22%)
  Pallas kernels  7.43 us (8%)
  waiting for transfers between devices  3.89 us (4%)
  matrix products  1.95 us (2%)
  other arithmetic  1.04 us (1%)
    all_to_all x1, blocking collectives, shards(): got = lax.all_to_all(send, FIRST + SECOND, 0, 0)  24.3 us
    ppermute x5, starting transfers between devices, flip(): return lax.ppermute(value, axis, [(0, 1), (1, 0)])  21.7 us
    all_to_all x1, blocking collectives, shards(): got = lax.all_to_all(send, FIRST, 0, 0)  21 us
    all_to_all x1, blocking collectives, shards(): got = lax.all_to_all(send, SECOND, 0, 0)  16.1 us
    pallas_call x1, Pallas kernels, shards(): call(factor_body, (shape(32, LANES), shape(32, LANES)), 2, 500000000, 100...  3.97 us
    ppermute x5, waiting for transfers between devices, flip(): return lax.ppermute(value, axis, [(0, 1), (1, 0)])  3.89 us
  transfers between devices with their start and end apart: 5, of which 3 were waited for; matrix products, arithmetic and copies ran while one was open for 2% of the time, Pallas kernels for 4%

profile of v5, /device:TPU:4, one launch (start us, length us, event | category | flops | bytes accessed | tf_op | source)
XLA Modules:
  0.0 98.1 jit_solution(7690887864543537500)
XLA Ops:
  0.6 0.0 copy-start
  0.6 1.0 %bitcast_convert_fusion = f32[16,5120]{1,0:T(8,128)S(1)} fusion(bf16[1,2,16,5120]{3,2,1,0:T(8,128)(2,1)} %param.3), kind=kLoop, calls=%fused_computation | loop fusion | flops 81920 | bytes 491520 | tf_op jit(solution)/shard_map/convert_element_type | solution.py:307
  1.7 1.9 %collective-permute-start = (f32[16,5120]{1,0:T(8,128)S(1)}, f32[16,5120]{1,0:T(8,128)S(1)}, u32[]{:S(2)}, u32[]{:S(2)}) collective-permute-start(f32[16,5120]{1,0:T(8,128)S(1)} %bitcast_convert_fusion), channel_id=1, source_target_pairs={{0,32},{32,0},{1,33},{33,1},{2,34},{34,2},{3,35},{35,3},{4,36},{36... | collective-permute-start | bytes 983048 | tf_op jit(solution)/shard_map/ppermute | solution.py:300
  3.6 1.9 %fusion.sketch_ref = f32[32,128]{1,0:T(8,128)S(1)} fusion(bf16[32,5120]{1,0:T(8,128)(2,1)} %bitcast.13, bf16[1,128,5120]{2,1,0:T(8,128)(2,1)} %param.2), kind=kOutput, calls=%fused_computation.1 | convolution fusion | flops 41943040 | bytes 1654784 | tf_op jit(solution)/shard_map/dot_general | solution.py:308
  5.6 0.0 collective-permute-done.starts_ref
  5.6 0.0 copy-done
  5.6 0.4 shard_map.41.mine_ref
  6.0 2.4 %collective-permute-start.1 = (f32[32,128]{1,0:T(8,128)S(1)}, f32[32,128]{1,0:T(8,128)S(1)}, u32[]{:S(2)}, u32[]{:S(2)}) collective-permute-start(f32[32,128]{1,0:T(8,128)S(1)} %shard_map.41.mine_ref), channel_id=1, source_target_pairs={{0,32},{32,0},{1,33},{33,1},{2,34},{34,2},{3,35},{35,3},{4,36},{36... | collective-permute-start | bytes 49160 | tf_op jit(solution)/shard_map/ppermute | solution.py:300
  8.5 0.8 collective-permute-done.1.side_ref
  9.3 7.7 %collective-permute-start.2 = (f32[48,128]{1,0:T(8,128)S(1)}, f32[48,128]{1,0:T(8,128)S(1)}, u32[]{:S(2)}, u32[]{:S(2)}) collective-permute-start(f32[48,128]{1,0:T(8,128)S(1)} %shard_map.42.mine_ref), channel_id=1, source_target_pairs={{0,256},{256,0},{1,257},{257,1},{2,258},{258,2},{3,259},{259,3},{4... | collective-permute-start | bytes 73736 | tf_op jit(solution)/shard_map/ppermute | solution.py:300
  17.0 1.9 %collective-permute-done.2.far_ref = f32[48,128]{1,0:T(8,128)S(1)} collective-permute-done((f32[48,128]{1,0:T(8,128)S(1)}, f32[48,128]{1,0:T(8,128)S(1)}, u32[]{:S(2)}, u32[]{:S(2)}) %collective-permute-start.2) | collective-permute-done | bytes 24608 | tf_op jit(solution)/shard_map/ppermute | solution.py:300
  18.9 0.6 shard_map.43
  19.5 21.0 %all_to_all.15.got_ref = f32[8,256,128]{2,1,0:T(8,128)S(1)} all-to-all(f32[8,256,128]{2,1,0:T(8,128)S(1)} %get-tuple-element.13), channel_id=1, replica_groups=mesh['h'=2,'y'=4,'c'=2,'x'=4,'w'=4,'v'=2] {'v','x'}, dimensions={0} | all-to-all | bytes 2097152 | tf_op jit(solution)/shard_map/all_to_all | solution.py:321
  40.5 0.1 shard_map.44
  40.6 16.1 %all_to_all.16.got_ref = f32[4,80,128]{2,1,0:T(8,128)S(1)} all-to-all(f32[4,80,128]{2,1,0:T(8,128)S(1)} %shard_map.44), channel_id=1, replica_groups=mesh['h'=2,'y'=4,'c'=2,'x'=4,'w'=4,'v'=2] {'w'}, dimensions={0} | all-to-all | bytes 327680 | tf_op jit(solution)/shard_map/all_to_all | solution.py:323
  56.8 1.9 %collective-permute-start.3 = (f32[32,128]{1,0:T(8,128)S(1)}, f32[32,128]{1,0:T(8,128)S(1)}, u32[]{:S(2)}, u32[]{:S(2)}) collective-permute-start(f32[32,128]{1,0:T(8,128)S(1)} %get-tuple-element.15), channel_id=1, source_target_pairs={{0,32},{32,0},{1,33},{33,1},{2,34},{34,2},{3,35},{35,3},{4,36},{36... | collective-permute-start | bytes 49160 | tf_op jit(solution)/shard_map/ppermute | solution.py:300
  58.7 1.1 %collective-permute-done.3.side_ref = f32[32,128]{1,0:T(8,128)S(1)} collective-permute-done((f32[32,128]{1,0:T(8,128)S(1)}, f32[32,128]{1,0:T(8,128)S(1)}, u32[]{:S(2)}, u32[]{:S(2)}) %collective-permute-start.3) | collective-permute-done | bytes 16416 | tf_op jit(solution)/shard_map/ppermute | solution.py:300
  59.8 0.1 shard_map.46
  59.9 7.7 %collective-permute-start.4 = (f32[80,128]{1,0:T(8,128)S(1)}, f32[80,128]{1,0:T(8,128)S(1)}, u32[]{:S(2)}, u32[]{:S(2)}) collective-permute-start(f32[80,128]{1,0:T(8,128)S(1)} %get-tuple-element.17), channel_id=1, source_target_pairs={{0,256},{256,0},{1,257},{257,1},{2,258},{258,2},{3,259},{259,3},{4... | collective-permute-start | bytes 122888 | tf_op jit(solution)/shard_map/ppermute | solution.py:300
  67.6 4.0 %shard_map.47 = (f32[32,128]{1,0:T(8,128)S(1)}, f32[32,128]{1,0:T(8,128)S(1)}) custom-call(f32[16,128]{1,0:T(8,128)S(1)} %get-tuple-element.18.gram_ref, f32[48,128]{1,0:T(8,128)S(1)} %get-tuple-element.19.stack_ref), custom_call_target="tpu_custom_call" | custom-call | flops 500000000 | bytes 10000000 | tf_op jit(solution)/shard_map/pallas_call | solution.py:330
  71.6 0.0 collective-permute-done.4.far_ref
  71.6 0.4 shard_map.48
  71.9 24.3 %all_to_all.17.got_ref = f32[32,40,128]{2,1,0:T(8,128)S(1)} all-to-all(f32[32,40,128]{2,1,0:T(8,128)S(1)} %shard_map.48), channel_id=1, replica_groups=mesh['h'=2,'y'=4,'c'=2,'x'=4,'w'=4,'v'=2] {'v','x','w'}, dimensions={0} | all-to-all | bytes 1310720 | tf_op jit(solution)/shard_map/all_to_all | solution.py:334
  96.2 1.9 %shard_map.49 = (bf16[128,5120]{1,0:T(8,128)(2,1)}, f32[2,16,5120]{2,1,0:T(8,128)}) custom-call(f32[32,40,128]{2,1,0:T(8,128)S(1)} %all_to_all.17.got_ref, bf16[128,5120]{1,0:T(8,128)(2,1)S(1)} %bitcast.12, f32[32,128]{1,0:T(8,128)S(1)} %get-tuple-element.21.basis_ref), custom_call_target="tpu_custom_call" | custom-call | tf_op jit(solution)/shard_map/pallas_call | solution.py:336
  (2 shorter events, 0.0 us)
Async XLA Ops:
  0.6 5.0 %copy-start = (bf16[1,128,5120]{2,1,0:T(8,128)(2,1)S(1)}, bf16[1,128,5120]{2,1,0:T(8,128)(2,1)}, u32[]{:S(2)}) copy-start(bf16[1,128,5120]{2,1,0:T(8,128)(2,1)} %param.2) | copy-start | bytes 3932164
  1.7 3.9 %collective-permute-start = (f32[16,5120]{1,0:T(8,128)S(1)}, f32[16,5120]{1,0:T(8,128)S(1)}, u32[]{:S(2)}, u32[]{:S(2)}) collective-permute-start(f32[16,5120]{1,0:T(8,128)S(1)} %bitcast_convert_fusion), channel_id=1, source_target_pairs={{0,32},{32,0},{1,33},{33,1},{2,34},{34,2},{3,35},{35,3},{4,36},{36... | collective-permute-start | bytes 983048 | tf_op jit(solution)/shard_map/ppermute | solution.py:300
  6.0 3.2 %collective-permute-start.1 = (f32[32,128]{1,0:T(8,128)S(1)}, f32[32,128]{1,0:T(8,128)S(1)}, u32[]{:S(2)}, u32[]{:S(2)}) collective-permute-start(f32[32,128]{1,0:T(8,128)S(1)} %shard_map.41.mine_ref), channel_id=1, source_target_pairs={{0,32},{32,0},{1,33},{33,1},{2,34},{34,2},{3,35},{35,3},{4,36},{36... | collective-permute-start | bytes 49160 | tf_op jit(solution)/shard_map/ppermute | solution.py:300
  9.3 9.6 %collective-permute-start.2 = (f32[48,128]{1,0:T(8,128)S(1)}, f32[48,128]{1,0:T(8,128)S(1)}, u32[]{:S(2)}, u32[]{:S(2)}) collective-permute-start(f32[48,128]{1,0:T(8,128)S(1)} %shard_map.42.mine_ref), channel_id=1, source_target_pairs={{0,256},{256,0},{1,257},{257,1},{2,258},{258,2},{3,259},{259,3},{4... | collective-permute-start | bytes 73736 | tf_op jit(solution)/shard_map/ppermute | solution.py:300
  56.8 3.1 %collective-permute-start.3 = (f32[32,128]{1,0:T(8,128)S(1)}, f32[32,128]{1,0:T(8,128)S(1)}, u32[]{:S(2)}, u32[]{:S(2)}) collective-permute-start(f32[32,128]{1,0:T(8,128)S(1)} %get-tuple-element.15), channel_id=1, source_target_pairs={{0,32},{32,0},{1,33},{33,1},{2,34},{34,2},{3,35},{35,3},{4,36},{36... | collective-permute-start | bytes 49160 | tf_op jit(solution)/shard_map/ppermute | solution.py:300
  59.9 11.7 %collective-permute-start.4 = (f32[80,128]{1,0:T(8,128)S(1)}, f32[80,128]{1,0:T(8,128)S(1)}, u32[]{:S(2)}, u32[]{:S(2)}) collective-permute-start(f32[80,128]{1,0:T(8,128)S(1)} %get-tuple-element.17), channel_id=1, source_target_pairs={{0,256},{256,0},{1,257},{257,1},{2,258},{258,2},{3,259},{259,3},{4... | collective-permute-start | bytes 122888 | tf_op jit(solution)/shard_map/ppermute | solution.py:300

commit v6 on v5

--- a/solution.py
+++ b/solution.py
@@ -253,14 +253,15 @@
     for x in range(4):
         tiles = []
         for first in range(x * FIRST_SIZE // 4, (x + 1) * FIRST_SIZE // 4):
-            base = first * SECOND_SIZE
-            tiles += [got_ref[base + z, 0:32, :] for z in range(SECOND_SIZE)]
+            v, x_index = first // 4, first % 4
+            owners = [v * 16 + w * 4 + x_index for w in range(SECOND_SIZE)]
+            tiles += [got_ref[owner, 0:32, :] for owner in owners]
             for k in range(REST):
                 groups = []
                 for a in range(4):
                     row = None
                     for g in range(4):
-                        piece = got_ref[base + 4 * k + g, 32:40, :]
+                        piece = got_ref[owners[4 * k + g], 32:40, :]
                         shift = (GROUP * (g - a)) % LANES
                         if shift:
                             piece = pltpu.roll(piece, shift, 1)
@@ -331,7 +332,7 @@
         factor_body, (shape(32, LANES), shape(32, LANES)), 2, 500_000_000, 10_000_000
     )(gram, stack)
     send = call(combine_body, shape(OWNERS, 40, LANES), 4)(sums, side, far, mix)
-    got = lax.all_to_all(send, FIRST + SECOND, 0, 0)
+    got = lax.all_to_all(send, ("v", "w", "x"), 0, 0)
     hbm = pl.BlockSpec(memory_space=pltpu.HBM)
     corrected, factors = pl.pallas_call(
         update_body,

time: 98.5 us -> 99.5 us (1.010)
  the two profiles are of different devices: /device:TPU:4 before, /device:TPU:64 now
where the time goes in v6:
time: 99.5 us; the launch traced here: 99.1 us
  blocking collectives  62.4 us (63%)
  starting transfers between devices  21.7 us (22%)
  Pallas kernels  7.43 us (7%)
  waiting for transfers between devices  3.89 us (4%)
  matrix products  1.95 us (2%)
  other arithmetic  1.04 us (1%)
    all_to_all x1, blocking collectives, shards(): got = lax.all_to_all(send, ('v', 'w', 'x'), 0, 0)  24.5 us
    ppermute x5, starting transfers between devices, flip(): return lax.ppermute(value, axis, [(0, 1), (1, 0)])  21.7 us
    all_to_all x1, blocking collectives, shards(): got = lax.all_to_all(send, FIRST, 0, 0)  21.3 us
    all_to_all x1, blocking collectives, shards(): got = lax.all_to_all(send, SECOND, 0, 0)  16.6 us
    pallas_call x1, Pallas kernels, shards(): call(factor_body, (shape(32, LANES), shape(32, LANES)), 2, 500000000, 100...  3.97 us
    ppermute x5, waiting for transfers between devices, flip(): return lax.ppermute(value, axis, [(0, 1), (1, 0)])  3.89 us
  transfers between devices with their start and end apart: 5, of which 3 were waited for; matrix products, arithmetic and copies ran while one was open for 2% of the time, Pallas kernels for 4%

profile of v6, /device:TPU:64, one launch (start us, length us, event | category | flops | bytes accessed | tf_op | source)
XLA Modules:
  0.0 99.1 jit_solution(18016930919613859920)
XLA Ops:
  0.6 0.0 copy-start
  0.6 1.0 %bitcast_convert_fusion = f32[16,5120]{1,0:T(8,128)S(1)} fusion(bf16[1,2,16,5120]{3,2,1,0:T(8,128)(2,1)} %param.3), kind=kLoop, calls=%fused_computation | loop fusion | flops 81920 | bytes 491520 | tf_op jit(solution)/shard_map/convert_element_type | solution.py:308
  1.7 1.9 %collective-permute-start = (f32[16,5120]{1,0:T(8,128)S(1)}, f32[16,5120]{1,0:T(8,128)S(1)}, u32[]{:S(2)}, u32[]{:S(2)}) collective-permute-start(f32[16,5120]{1,0:T(8,128)S(1)} %bitcast_convert_fusion), channel_id=1, source_target_pairs={{0,32},{32,0},{1,33},{33,1},{2,34},{34,2},{3,35},{35,3},{4,36},{36... | collective-permute-start | bytes 983048 | tf_op jit(solution)/shard_map/ppermute | solution.py:301
  3.6 1.9 %fusion.sketch_ref = f32[32,128]{1,0:T(8,128)S(1)} fusion(bf16[32,5120]{1,0:T(8,128)(2,1)} %bitcast.13, bf16[1,128,5120]{2,1,0:T(8,128)(2,1)} %param.2), kind=kOutput, calls=%fused_computation.1 | convolution fusion | flops 41943040 | bytes 1654784 | tf_op jit(solution)/shard_map/dot_general | solution.py:309
  5.6 0.0 collective-permute-done.starts_ref
  5.6 0.0 copy-done
  5.6 0.4 shard_map.41.mine_ref
  6.0 2.4 %collective-permute-start.1 = (f32[32,128]{1,0:T(8,128)S(1)}, f32[32,128]{1,0:T(8,128)S(1)}, u32[]{:S(2)}, u32[]{:S(2)}) collective-permute-start(f32[32,128]{1,0:T(8,128)S(1)} %shard_map.41.mine_ref), channel_id=1, source_target_pairs={{0,32},{32,0},{1,33},{33,1},{2,34},{34,2},{3,35},{35,3},{4,36},{36... | collective-permute-start | bytes 49160 | tf_op jit(solution)/shard_map/ppermute | solution.py:301
  8.5 0.8 collective-permute-done.1.side_ref
  9.3 7.7 %collective-permute-start.2 = (f32[48,128]{1,0:T(8,128)S(1)}, f32[48,128]{1,0:T(8,128)S(1)}, u32[]{:S(2)}, u32[]{:S(2)}) collective-permute-start(f32[48,128]{1,0:T(8,128)S(1)} %shard_map.42.mine_ref), channel_id=1, source_target_pairs={{0,256},{256,0},{1,257},{257,1},{2,258},{258,2},{3,259},{259,3},{4... | collective-permute-start | bytes 73736 | tf_op jit(solution)/shard_map/ppermute | solution.py:301
  17.0 1.9 %collective-permute-done.2.far_ref = f32[48,128]{1,0:T(8,128)S(1)} collective-permute-done((f32[48,128]{1,0:T(8,128)S(1)}, f32[48,128]{1,0:T(8,128)S(1)}, u32[]{:S(2)}, u32[]{:S(2)}) %collective-permute-start.2) | collective-permute-done | bytes 24608 | tf_op jit(solution)/shard_map/ppermute | solution.py:301
  18.9 0.6 shard_map.43
  19.5 21.3 %all_to_all.15.got_ref = f32[8,256,128]{2,1,0:T(8,128)S(1)} all-to-all(f32[8,256,128]{2,1,0:T(8,128)S(1)} %get-tuple-element.13), channel_id=1, replica_groups=mesh['h'=2,'y'=4,'c'=2,'x'=4,'w'=4,'v'=2] {'v','x'}, dimensions={0} | all-to-all | bytes 2097152 | tf_op jit(solution)/shard_map/all_to_all | solution.py:322
  40.9 0.1 shard_map.44
  41.0 16.6 %all_to_all.16.got_ref = f32[4,80,128]{2,1,0:T(8,128)S(1)} all-to-all(f32[4,80,128]{2,1,0:T(8,128)S(1)} %shard_map.44), channel_id=1, replica_groups=mesh['h'=2,'y'=4,'c'=2,'x'=4,'w'=4,'v'=2] {'w'}, dimensions={0} | all-to-all | bytes 327680 | tf_op jit(solution)/shard_map/all_to_all | solution.py:324
  57.6 1.9 %collective-permute-start.3 = (f32[32,128]{1,0:T(8,128)S(1)}, f32[32,128]{1,0:T(8,128)S(1)}, u32[]{:S(2)}, u32[]{:S(2)}) collective-permute-start(f32[32,128]{1,0:T(8,128)S(1)} %get-tuple-element.15), channel_id=1, source_target_pairs={{0,32},{32,0},{1,33},{33,1},{2,34},{34,2},{3,35},{35,3},{4,36},{36... | collective-permute-start | bytes 49160 | tf_op jit(solution)/shard_map/ppermute | solution.py:301
  59.6 1.1 %collective-permute-done.3.side_ref = f32[32,128]{1,0:T(8,128)S(1)} collective-permute-done((f32[32,128]{1,0:T(8,128)S(1)}, f32[32,128]{1,0:T(8,128)S(1)}, u32[]{:S(2)}, u32[]{:S(2)}) %collective-permute-start.3) | collective-permute-done | bytes 16416 | tf_op jit(solution)/shard_map/ppermute | solution.py:301
  60.7 0.1 shard_map.46
  60.8 7.7 %collective-permute-start.4 = (f32[80,128]{1,0:T(8,128)S(1)}, f32[80,128]{1,0:T(8,128)S(1)}, u32[]{:S(2)}, u32[]{:S(2)}) collective-permute-start(f32[80,128]{1,0:T(8,128)S(1)} %get-tuple-element.17), channel_id=1, source_target_pairs={{0,256},{256,0},{1,257},{257,1},{2,258},{258,2},{3,259},{259,3},{4... | collective-permute-start | bytes 122888 | tf_op jit(solution)/shard_map/ppermute | solution.py:301
  68.5 4.0 %shard_map.47 = (f32[32,128]{1,0:T(8,128)S(1)}, f32[32,128]{1,0:T(8,128)S(1)}) custom-call(f32[16,128]{1,0:T(8,128)S(1)} %get-tuple-element.18.gram_ref, f32[48,128]{1,0:T(8,128)S(1)} %get-tuple-element.19.stack_ref), custom_call_target="tpu_custom_call" | custom-call | flops 500000000 | bytes 10000000 | tf_op jit(solution)/shard_map/pallas_call | solution.py:331
  72.4 0.0 collective-permute-done.4.far_ref
  72.4 0.4 shard_map.48
  72.8 24.5 %all_to_all.17.got_ref = f32[32,40,128]{2,1,0:T(8,128)S(1)} all-to-all(f32[32,40,128]{2,1,0:T(8,128)S(1)} %shard_map.48), channel_id=1, replica_groups=mesh['h'=2,'y'=4,'c'=2,'x'=4,'w'=4,'v'=2] {'v','w','x'}, dimensions={0} | all-to-all | bytes 1310720 | tf_op jit(solution)/shard_map/all_to_all | solution.py:335
  97.3 1.9 %shard_map.49 = (bf16[128,5120]{1,0:T(8,128)(2,1)}, f32[2,16,5120]{2,1,0:T(8,128)}) custom-call(f32[32,40,128]{2,1,0:T(8,128)S(1)} %all_to_all.17.got_ref, bf16[128,5120]{1,0:T(8,128)(2,1)S(1)} %bitcast.12, f32[32,128]{1,0:T(8,128)S(1)} %get-tuple-element.21.basis_ref), custom_call_target="tpu_custom_call" | custom-call | tf_op jit(solution)/shard_map/pallas_call | solution.py:337
  (2 shorter events, 0.0 us)
Async XLA Ops:
  0.6 5.0 %copy-start = (bf16[1,128,5120]{2,1,0:T(8,128)(2,1)S(1)}, bf16[1,128,5120]{2,1,0:T(8,128)(2,1)}, u32[]{:S(2)}) copy-start(bf16[1,128,5120]{2,1,0:T(8,128)(2,1)} %param.2) | copy-start | bytes 3932164
  1.7 3.9 %collective-permute-start = (f32[16,5120]{1,0:T(8,128)S(1)}, f32[16,5120]{1,0:T(8,128)S(1)}, u32[]{:S(2)}, u32[]{:S(2)}) collective-permute-start(f32[16,5120]{1,0:T(8,128)S(1)} %bitcast_convert_fusion), channel_id=1, source_target_pairs={{0,32},{32,0},{1,33},{33,1},{2,34},{34,2},{3,35},{35,3},{4,36},{36... | collective-permute-start | bytes 983048 | tf_op jit(solution)/shard_map/ppermute | solution.py:301
  6.0 3.2 %collective-permute-start.1 = (f32[32,128]{1,0:T(8,128)S(1)}, f32[32,128]{1,0:T(8,128)S(1)}, u32[]{:S(2)}, u32[]{:S(2)}) collective-permute-start(f32[32,128]{1,0:T(8,128)S(1)} %shard_map.41.mine_ref), channel_id=1, source_target_pairs={{0,32},{32,0},{1,33},{33,1},{2,34},{34,2},{3,35},{35,3},{4,36},{36... | collective-permute-start | bytes 49160 | tf_op jit(solution)/shard_map/ppermute | solution.py:301
  9.3 9.6 %collective-permute-start.2 = (f32[48,128]{1,0:T(8,128)S(1)}, f32[48,128]{1,0:T(8,128)S(1)}, u32[]{:S(2)}, u32[]{:S(2)}) collective-permute-start(f32[48,128]{1,0:T(8,128)S(1)} %shard_map.42.mine_ref), channel_id=1, source_target_pairs={{0,256},{256,0},{1,257},{257,1},{2,258},{258,2},{3,259},{259,3},{4... | collective-permute-start | bytes 73736 | tf_op jit(solution)/shard_map/ppermute | solution.py:301
  57.6 3.1 %collective-permute-start.3 = (f32[32,128]{1,0:T(8,128)S(1)}, f32[32,128]{1,0:T(8,128)S(1)}, u32[]{:S(2)}, u32[]{:S(2)}) collective-permute-start(f32[32,128]{1,0:T(8,128)S(1)} %get-tuple-element.15), channel_id=1, source_target_pairs={{0,32},{32,0},{1,33},{33,1},{2,34},{34,2},{3,35},{35,3},{4,36},{36... | collective-permute-start | bytes 49160 | tf_op jit(solution)/shard_map/ppermute | solution.py:301
  60.8 11.7 %collective-permute-start.4 = (f32[80,128]{1,0:T(8,128)S(1)}, f32[80,128]{1,0:T(8,128)S(1)}, u32[]{:S(2)}, u32[]{:S(2)}) collective-permute-start(f32[80,128]{1,0:T(8,128)S(1)} %get-tuple-element.17), channel_id=1, source_target_pairs={{0,256},{256,0},{1,257},{257,1},{2,258},{258,2},{3,259},{259,3},{4... | collective-permute-start | bytes 122888 | tf_op jit(solution)/shard_map/ppermute | solution.py:301
